TPU v7x, 512 devices: a whole 4x8x8 slice. The times are simulated.
512 devices in a mesh: tm: 8 (over x, y_hi), space: 64 (over z, y_lo, core).
Axes of the slice: x: 4, y: 8 (y_hi: 2, y_lo: 4; y = y_hi * 4 + y_lo), z: 8, core: 2. Of those that a mesh axis runs over, the one named last changes fastest.
Arguments:
- adjoint: float32 [8, 5, 256, 1024], P('tm', None, 'space'), may hold values from -6 to 6
- jac_x: float32 [8, 4, 5, 5, 256, 1024], P('tm', None, None, None, 'space'), may hold values from -4 to 4
- jac_local: float32 [8, 3, 5, 5, 256, 1024], P('tm', None, None, None, 'space'), may hold values from -4 to 4
- objective_gradient: float32 [8, 5, 256, 1024], P('tm', None, 'space'), may hold values from -6 to 6
- volume: float32 [256, 1024], P('space'), may hold values from 0.5 to 2
- face_lower: int32 [64, 1024], P('space'), may hold values from 0 to 1023, as said below
- face_upper: int32 [64, 1024], P('space'), may hold values from 0 to 1023, as said below
Outputs:
- adjoint_residual: float32 [8, 5, 256, 1024], P('tm', None, 'space')
Inputs may be any that keep to these rules, and one draw needn't show every extreme that they name: `face_lower`: each row is a permutation of 0 to 1023; row 0 is never read. `face_upper`: each row is a permutation of 0 to 1023, and row s is the inverse permutation of face_lower row s+1 (the last row that of row 0, and never read).
All inputs are finite; a program needn't handle non-finite values.
Results may differ from a plain program's by a relative error of at most 0.000065.
Values sent between devices are 32-bit elements; how exact they have to be, the bound alone decides.
No kernel may reach another device: no remote copies, remote signals or barrier semaphores. Data moves between devices by JAX's collectives and lax.ppermute only.
A program may use at most 64 MiB of HBM per device.

v0:
```python
import jax
import jax.numpy as jnp
from jax import lax
from jax.sharding import PartitionSpec as P

NT = 8
NF = 5


def extended_2(block, sides, width):
    for axis, dim in sides:
        count = lax.axis_size(axis)
        forward = [(i, i + 1) for i in range(count - 1)]
        backward = [(target, source) for source, target in forward]
        low = lax.ppermute(
            lax.slice_in_dim(block, block.shape[dim] - width, None, axis=dim), axis, forward
        )
        high = lax.ppermute(lax.slice_in_dim(block, 0, width, axis=dim), axis, backward)
        block = jnp.concatenate([low, block, high], axis=dim)
    return block


def spectral_table(count):
    index = jnp.arange(count)
    offset = index[:, None] - index[None, :]
    parity = jnp.where(offset % 2 == 0, 1.0, -1.0).astype(jnp.float32)
    mask = jnp.logical_and(offset != 0, jnp.abs(offset) * 2 != count)
    safe = jnp.where(mask, offset, 1).astype(jnp.float32)
    first = jnp.where(mask, 0.5 * parity / jnp.tan(jnp.pi * safe / count), 0.0)
    apart = offset != 0
    wide = jnp.where(apart, offset, 1).astype(jnp.float32)
    sine = jnp.sin(jnp.pi * wide / count)
    second = jnp.where(apart, -0.5 * parity / (sine * sine), -(count * count + 2) / 12.0)
    return first + 0.25 * second


def match_faces(extended, face_lower, face_upper):
    lower = jnp.take(extended[:, :, :2], face_lower[0], axis=3)
    upper = jnp.take(extended[:, :, -2:], face_upper[0], axis=3)
    return jnp.concatenate([lower, extended[:, :, 2:-2], upper], axis=2)


def transposed(blocks, fields):
    return jnp.sum(blocks * fields[:, None, :, None], axis=2)


def offset_sum(q_terms, layers):
    xpart = None
    for k_index, offset in enumerate((1, -1, 2, -2)):
        piece = q_terms[:, k_index, :, 2 - offset : 2 - offset + layers, :]
        xpart = piece if xpart is None else xpart + piece
    return xpart


def body(adjoint, jac_x, jac_local, objective_gradient, volume, face_lower, face_upper):
    steps_here = adjoint.shape[0]
    layers = adjoint.shape[2]
    cells = adjoint.shape[3]
    joined = jnp.concatenate([adjoint, jac_x.reshape(steps_here, 100, layers, cells)], axis=1)
    extended = extended_2(joined, (("space", 2),), 2)
    extended = match_faces(extended, face_lower, face_upper)
    q_terms = transposed(
        extended[:, NF:].reshape(steps_here, 4, NF, NF, layers + 4, cells), extended[:, :NF]
    )
    xpart = offset_sum(q_terms, layers)
    center = jnp.sum(jac_local[:, 0] * adjoint[:, :, None], axis=1)
    plus_term = jnp.sum(jac_local[:, 1] * adjoint[:, :, None], axis=1)
    minus_term = jnp.sum(jac_local[:, 2] * adjoint[:, :, None], axis=1)
    zero_col = jnp.zeros((steps_here, NF, layers, 1), adjoint.dtype)
    from_below = jnp.concatenate([zero_col, plus_term[..., :-1]], axis=3)
    from_above = jnp.concatenate([minus_term[..., 1:], zero_col], axis=3)
    local = center + from_below + from_above
    table = spectral_table(NT)
    own_start = lax.axis_index("tm") * steps_here
    own_columns = lax.dynamic_slice_in_dim(table, own_start, steps_here, 1)
    spectral = jnp.einsum(
        "st,sfxy->tfxy",
        own_columns,
        lax.all_gather(adjoint, "tm", axis=0, tiled=True),
        precision=lax.Precision.HIGHEST,
    )
    return objective_gradient + local + xpart + 1.5 * volume[None, None] * spectral


def solution(mesh):
    in_specs = (
        P("tm", None, "space", None),
        P("tm", None, None, None, "space", None),
        P("tm", None, None, None, "space", None),
        P("tm", None, "space", None),
        P("space", None),
        P("space", None),
        P("space", None),
    )
    out_specs = P("tm", None, "space", None)
    return jax.shard_map(body, mesh=mesh, in_specs=in_specs, out_specs=out_specs, check_vma=False)
```

profile of v0, /device:TPU:392, one launch (start us, length us, event | category | flops | bytes accessed | tf_op | source)
XLA Modules:
  0.0 114.8 jit_solution(15808425995703130289)
XLA Ops:
  0.0 0.0 copy-start.1
  0.0 0.0 copy-start.10
  0.0 0.0 copy-start.12
  0.0 0.0 copy-start.3
  0.0 3.9 %fusion = (f32[1,105,2,1024]{3,2,1,0:T(2,128)S(1)}, f32[1,105,2,1024]{3,2,1,0:T(2,128)}) fusion(f32[1,5,4,1024]{3,2,1,0:T(4,128)} %param.9, f32[1,100,4,1024]{3,2,1,0:T(4,128)} %bitcast.60), kind=kLoop, calls=%fused_computation.8 | loop fusion | flops 430080 | bytes 3440640 | tf_op jit(solution)/shard_map/concatenate | solution.py:59
  3.9 1.9 %collective-permute-start = (f32[1,105,2,1024]{3,2,1,0:T(2,128)S(1)}, f32[1,105,2,1024]{3,2,1,0:T(2,128)S(1)}, u32[]{:S(2)}, u32[]{:S(2)}) collective-permute-start(f32[1,105,2,1024]{3,2,1,0:T(2,128)S(1)} %get-tuple-element.9), channel_id=1, source_target_pairs={{0,1},{1,2},{2,3},{3,4},{4,5},{5,6},{6,7},{7,8},{8,9},{9,10},{10,1... | collective-permute-start | bytes 2580488 | tf_op jit(solution)/shard_map/ppermute | solution.py:15
  5.9 3.6 %collective-permute-start.1 = (f32[1,105,2,1024]{3,2,1,0:T(2,128)}, f32[1,105,2,1024]{3,2,1,0:T(2,128)}, u32[]{:S(2)}, u32[]{:S(2)}) collective-permute-start(f32[1,105,2,1024]{3,2,1,0:T(2,128)} %get-tuple-element.10), channel_id=1, source_target_pairs={{1,0},{2,1},{3,2},{4,3},{5,4},{6,5},{7,6},{8,7},{9,8},{10,9},{11,1... | collective-permute-start | bytes 2580488 | tf_op jit(solution)/shard_map/ppermute | solution.py:18
  9.5 0.0 copy-done.10
  9.5 0.0 copy-done.11
  9.6 0.0 copy-done.12
  9.6 0.6 broadcast_multiply_fusion
  10.2 0.0 copy-done.1
  10.2 0.0 copy-done.3
  10.2 1.0 fusion.4
  11.2 0.1 fusion.13
  11.3 0.7 slice.57
  12.0 69.2 %all_gather.3 = f32[8,5,4,1024]{3,2,1,0:T(4,128)S(1)} all-gather(f32[1,5,4,1024]{3,2,1,0:T(4,128)S(1)} %copy-done.1), channel_id=1, replica_groups=mesh['tm'=8,'space'=64] {'tm'}, dimensions={0}, use_global_device_ids=true | all-gather | bytes 737280 | tf_op jit(solution)/shard_map/all_gather | solution.py:79
  81.3 1.6 %fusion.1 = f32[1,5,4,1024]{3,0,2,1:T(1,128)} fusion(f32[8,5,4,1024]{3,2,1,0:T(4,128)S(1)} %all_gather.3, f32[8,8]{0,1:T(8,128)S(1)} %fusion.13, s32[]{:T(128)S(6)} %select_n.49), kind=kOutput, calls=%fused_computation.10 | convolution fusion | flops 1966080 | bytes 737796 | tf_op jit(solution)/shard_map/st,sfxy->tfxy/dot_general | solution.py:76
  82.9 0.0 collective-permute-done
  82.9 1.2 %copy.14 = f32[1,105,2,1024]{1,2,3,0:T(2,128)S(1)} copy(f32[1,105,2,1024]{3,2,1,0:T(2,128)S(1)} %collective-permute-done) | data formatting | bytes 1720320 | tf_op jit(solution)/shard_map/ppermute | solution.py:15
  84.1 3.6 %gather_fusion = f32[1024,105,2]{1,2,0:T(2,128)S(1)} fusion(f32[105,2,1024]{0,1,2:T(2,128)S(1)} %bitcast.64, s32[1024]{0:T(1024)S(1)} %fusion.26), kind=kCustom, calls=%fused_computation.clone | custom fusion | bytes 1724416 | tf_op jit(solution)/shard_map/jit(_take)/gather | solution.py:38
  87.7 3.7 %bitcast_select_fusion.1 = f32[1,105,2,1024]{1,2,3,0:T(2,128)S(1)} fusion(f32[1024,105,2]{1,2,0:T(2,128)S(1)} %gather_fusion, pred[1024]{0:T(1024)(128)(4,1)S(1)} %compare_and_fusion.2), kind=kLoop, calls=%fused_computation.7 | loop fusion | flops 215040 | bytes 1721344 | tf_op jit(solution)/shard_map/jit(_take)/select_n | solution.py:38
  91.4 1.2 %copy.16 = f32[1,105,2,1024]{3,2,1,0:T(2,128)S(1)} copy(f32[1,105,2,1024]{1,2,3,0:T(2,128)S(1)} %bitcast_select_fusion.1) | data formatting | bytes 1720320 | tf_op jit(solution)/shard_map/jit(_take)/select_n | solution.py:38
  92.7 0.0 collective-permute-done.1
  92.7 2.6 %copy.15 = f32[1,105,2,1024]{1,2,3,0:T(2,128)S(1)} copy(f32[1,105,2,1024]{3,2,1,0:T(2,128)} %collective-permute-done.1) | data formatting | bytes 1720320 | tf_op jit(solution)/shard_map/ppermute | solution.py:18
  95.3 0.0 copy-start
  95.3 7.5 %gather_fusion.1 = f32[1024,105,2]{1,2,0:T(2,128)} fusion(f32[105,2,1024]{0,1,2:T(2,128)S(1)} %bitcast.65, s32[1024]{0:T(1024)S(1)} %fusion.27), kind=kCustom, calls=%fused_computation.1.clone | custom fusion | bytes 1724416 | tf_op jit(solution)/shard_map/jit(_take)/gather | solution.py:39
  102.8 6.1 %bitcast_select_fusion = f32[1,105,2,1024]{1,2,3,0:T(2,128)} fusion(f32[1024,105,2]{1,2,0:T(2,128)} %gather_fusion.1, pred[1024]{0:T(1024)(128)(4,1)S(1)} %compare_and_fusion.1), kind=kLoop, calls=%fused_computation.6 | loop fusion | flops 215040 | bytes 1721344 | tf_op jit(solution)/shard_map/jit(_take)/select_n | solution.py:39
  108.9 2.4 %copy.17 = f32[1,105,2,1024]{3,2,1,0:T(2,128)S(1)} copy(f32[1,105,2,1024]{1,2,3,0:T(2,128)} %bitcast_select_fusion) | data formatting | bytes 1720320 | tf_op jit(solution)/shard_map/jit(_take)/select_n | solution.py:39
  111.3 0.0 copy-done
  111.4 0.0 copy-done.2
  111.4 0.1 maximum_bitcast_fusion
  111.4 1.1 pad_maximum_fusion
  112.6 0.4 slice.60
  113.0 0.0 copy-start.4
  113.0 0.0 copy-start.5
  113.0 0.0 copy-start.6
  113.0 0.0 copy-start.7
  113.0 0.0 copy-start.8
  113.0 0.0 copy-start.9
  113.0 0.4 multiply_reduce_fusion
  113.5 0.4 copy-done.4
  113.9 0.0 copy-done.5
  113.9 0.0 copy-done.6
  114.0 0.0 copy-done.7
  114.0 0.0 copy-done.8
  114.0 0.0 copy-done.9
  114.0 0.8 fusion.8
  (6 shorter events, 0.0 us)
Async XLA Ops:
  0.0 10.2 %copy-start.1 = (f32[1,5,4,1024]{3,2,1,0:T(4,128)S(1)}, f32[1,5,4,1024]{3,2,1,0:T(4,128)}, u32[]{:S(2)}) copy-start(f32[1,5,4,1024]{3,2,1,0:T(4,128)} %param.9) | copy-start | bytes 245764
  0.0 9.5 %copy-start.10 = (s32[1,1024]{1,0:T(1,128)S(1)}, s32[1,1024]{1,0:T(1,128)}, u32[]{:S(2)}) copy-start(s32[1,1024]{1,0:T(1,128)} %param.14) | copy-start | bytes 12292
  0.0 9.5 %copy-start.11 = (s32[1,1024]{1,0:T(1,128)S(1)}, s32[1,1024]{1,0:T(1,128)}, u32[]{:S(2)}) copy-start(s32[1,1024]{1,0:T(1,128)} %param.15) | copy-start | bytes 12292
  0.0 9.6 %copy-start.12 = (f32[4,1024]{1,0:T(4,128)S(1)}, f32[4,1024]{1,0:T(4,128)}, u32[]{:S(2)}) copy-start(f32[4,1024]{1,0:T(4,128)} %param.13) | copy-start | bytes 49156
  0.0 10.2 %copy-start.3 = (f32[1,3,5,5,4,1024]{5,4,3,2,1,0:T(4,128)S(1)}, f32[1,3,5,5,4,1024]{5,4,3,2,1,0:T(4,128)}, u32[]{:S(2)}) copy-start(f32[1,3,5,5,4,1024]{5,4,3,2,1,0:T(4,128)} %param.11) | copy-start | bytes 3686404
  3.9 78.9 %collective-permute-start = (f32[1,105,2,1024]{3,2,1,0:T(2,128)S(1)}, f32[1,105,2,1024]{3,2,1,0:T(2,128)S(1)}, u32[]{:S(2)}, u32[]{:S(2)}) collective-permute-start(f32[1,105,2,1024]{3,2,1,0:T(2,128)S(1)} %get-tuple-element.9), channel_id=1, source_target_pairs={{0,1},{1,2},{2,3},{3,4},{4,5},{5,6},{6,7},{7,8},{8,9},{9,10},{10,1... | collective-permute-start | bytes 2580488 | tf_op jit(solution)/shard_map/ppermute | solution.py:15
  5.9 86.8 %collective-permute-start.1 = (f32[1,105,2,1024]{3,2,1,0:T(2,128)}, f32[1,105,2,1024]{3,2,1,0:T(2,128)}, u32[]{:S(2)}, u32[]{:S(2)}) collective-permute-start(f32[1,105,2,1024]{3,2,1,0:T(2,128)} %get-tuple-element.10), channel_id=1, source_target_pairs={{1,0},{2,1},{3,2},{4,3},{5,4},{6,5},{7,6},{8,7},{9,8},{10,9},{11,1... | collective-permute-start | bytes 2580488 | tf_op jit(solution)/shard_map/ppermute | solution.py:18
  95.3 16.1 %copy-start = (f32[1,4,5,5,4,1024]{5,4,3,2,1,0:T(4,128)S(1)}, f32[1,4,5,5,4,1024]{5,4,3,2,1,0:T(4,128)}, u32[]{:S(2)}) copy-start(f32[1,4,5,5,4,1024]{5,4,3,2,1,0:T(4,128)} %param.10) | copy-start | bytes 4915204
  102.8 8.6 %copy-start.2 = (f32[1,5,4,1024]{3,2,1,0:T(4,128)S(1)}, f32[1,5,4,1024]{3,2,1,0:T(4,128)}, u32[]{:S(2)}) copy-start(f32[1,5,4,1024]{3,2,1,0:T(4,128)} %param.9) | copy-start | bytes 245764
  113.0 0.9 copy-start.4
  113.0 0.9 copy-start.5
  113.0 1.0 copy-start.6
  113.0 1.0 copy-start.7
  113.0 1.0 copy-start.8
  113.0 1.0 copy-start.9
where the time goes:
time: 115 us
  blocking collectives  69.2 us (60%)
  local copies, waits for them, and re-layouts  20.3 us (18%)
  other arithmetic  17.8 us (15%)
  starting transfers between devices  5.55 us (5%)
  matrix products  1.61 us (1%)
    all_gather x1, blocking collectives, body(): lax.all_gather(adjoint, 'tm', axis=0, tiled=True)  69.2 us
    gather x1, local copies, waits for them, and re-layouts, match_faces(): upper = jnp.take(extended[:, :, -2:], face_upper[0], axis=3)  7.47 us
    select_n x1, other arithmetic, match_faces(): upper = jnp.take(extended[:, :, -2:], face_upper[0], axis=3)  6.11 us
    concatenate x1, other arithmetic, body(): jnp.concatenate([adjoint, jac_x.reshape(steps_here, 100, layers, cells)],...  3.9 us
    select_n x1, other arithmetic, match_faces(): lower = jnp.take(extended[:, :, :2], face_lower[0], axis=3)  3.74 us
    ppermute x1, starting transfers between devices, extended_2(): lax.ppermute(lax.slice_in_dim(block, 0, width, axis=dim), axis, backward)  3.64 us
    gather x1, local copies, waits for them, and re-layouts, match_faces(): lower = jnp.take(extended[:, :, :2], face_lower[0], axis=3)  3.56 us
    ppermute x1, local copies, waits for them, and re-layouts, extended_2(): lax.ppermute(lax.slice_in_dim(block, 0, width, axis=dim), axis, backward)  2.58 us
  transfers between devices with their start and end apart: 2, of which 0 were waited for; matrix products, arithmetic and copies ran while one was open for 12% of the time, Pallas kernels for 0%

commit v1 on v0

v1 whole, which is shorter than its diff:
```python
import jax
import jax.numpy as jnp
import numpy as np
from jax import lax
from jax.experimental import pallas as pl
from jax.experimental.pallas import tpu as pltpu
from jax.sharding import PartitionSpec as P

NT = 8
NF = 5
PAIRS = NT // 2
VMEM = pl.BlockSpec(memory_space=pltpu.VMEM)
SMEM = pl.BlockSpec(memory_space=pltpu.SMEM)
ANY = pl.BlockSpec(memory_space=pl.ANY)


def spectral_table(count):
    index = np.arange(count)
    offset = index[:, None] - index[None, :]
    parity = np.where(offset % 2 == 0, 1.0, -1.0)
    mask = np.logical_and(offset != 0, np.abs(offset) * 2 != count)
    safe = np.where(mask, offset, 1)
    first = np.where(mask, 0.5 * parity / np.tan(np.pi * safe / count), 0.0)
    apart = offset != 0
    wide = np.where(apart, offset, 1)
    sine = np.sin(np.pi * wide / count)
    second = np.where(apart, -0.5 * parity / (sine * sine), -(count * count + 2) / 12.0)
    return (first + 0.25 * second).astype(np.float32)


def stencil_kernel(space_ref, adj_ref, jx_hbm, jl_hbm, obj_ref, part_ref, near_ref, far_ref,
                   jx, jl, ext, side, sems):
    copies = [pltpu.make_async_copy(jx_hbm.at[k], jx.at[k], sems.at[k]) for k in range(4)]
    copies += [pltpu.make_async_copy(jl_hbm.at[k], jl.at[k], sems.at[4 + k]) for k in range(3)]
    for copy in copies:
        copy.start()
    cells = adj_ref.shape[2]
    ext[...] = jnp.zeros_like(ext)
    side[...] = jnp.zeros_like(side)
    for k, offset in enumerate((1, -1, 2, -2)):
        copies[k].wait()
        for b in range(NF):
            q = jx[k, 0, b] * adj_ref[0]
            for a in range(1, NF):
                q = q + jx[k, a, b] * adj_ref[a]
            ext[b, 2 + offset:6 + offset, :] += q
    even = space_ref[0] % 2 == 0
    for b in range(NF):
        below = ext[b, 0:2, :]
        above = ext[b, 6:8, :]
        near_ref[b] = jnp.where(even, above, below)
        far_ref[b] = jnp.where(even, below, above)
    lane = lax.broadcasted_iota(jnp.int32, (8, cells), 1)
    for k in range(3):
        copies[4 + k].wait()
        for b in range(NF):
            q = jl[k, 0, b] * adj_ref[0]
            for a in range(1, NF):
                q = q + jl[k, a, b] * adj_ref[a]
            if k == 0:
                ext[b, 2:6, :] += q
            else:
                side[b, 2:6, :] = q
                moved = pltpu.roll(side[b], 1 if k == 1 else cells - 1, 1)
                ext[b] += jnp.where(lane == (0 if k == 1 else cells - 1), 0.0, moved)
    for b in range(NF):
        part_ref[b] = obj_ref[b] + ext[b, 2:6, :]


def combine_kernel(coef_ref, own_ref, other_ref, out_ref):
    for j in range(PAIRS):
        out_ref[j] = coef_ref[0, j] * own_ref[...] + coef_ref[1, j] * other_ref[...]


def finish_kernel(space_ref, part_ref, spec_ref, vol_ref, near_ref, far_ref, low_ref, up_ref, out_ref, halo, moved):
    odd = space_ref[0] % 2 == 1
    cells = vol_ref.shape[1]
    halo[...] = jnp.zeros_like(halo)
    for b in range(NF):
        row = 4 * (b % 2)
        halo[b // 2, row:row + 2, :] = jnp.where(odd, near_ref[b], far_ref[b])
        halo[b // 2, row + 2:row + 4, :] = jnp.where(odd, far_ref[b], near_ref[b])
    groups = halo.shape[0]
    chunks = cells // 128
    from_low = lax.broadcasted_iota(jnp.int32, (8, 128), 0) % 4 < 2
    for j in range(chunks):
        here = slice(128 * j, 128 * (j + 1))
        low = jnp.broadcast_to(low_ref[0:1, here], (8, 128))
        up = jnp.broadcast_to(up_ref[0:1, here], (8, 128))
        index = jnp.where(from_low, low, up)
        lane = index % 128
        chunk = index // 128
        for g in range(groups):
            total = None
            for c in range(chunks):
                piece = jnp.take_along_axis(halo[g, :, 128 * c:128 * (c + 1)], lane, axis=1, mode="promise_in_bounds")
                total = piece if c == 0 else jnp.where(chunk == c, piece, total)
            moved[g, :, here] = total
    scale = 1.5 * vol_ref[...]
    for b in range(NF):
        row = 4 * (b % 2)
        spectral = spec_ref[0, b]
        for j in range(1, PAIRS):
            spectral = spectral + spec_ref[j, b]
        out_ref[b] = part_ref[b] + moved[b // 2, row:row + 4, :] + scale * spectral


def body(adjoint, jac_x, jac_local, objective_gradient, volume, face_lower, face_upper):
    _, _, layers, cells = adjoint.shape
    space = lax.axis_index("space")
    here = lax.axis_index("tm")
    count = lax.axis_size("space")
    field = jax.ShapeDtypeStruct((NF, layers, cells), jnp.float32)
    face = jax.ShapeDtypeStruct((NF, 2, cells), jnp.float32)
    own = adjoint[0]
    other = lax.ppermute(own, "tm", [(i, i ^ 1) for i in range(NT)])
    space_at = space.reshape(1).astype(jnp.int32)
    part, near, far = pl.pallas_call(
        stencil_kernel,
        out_shape=(field, face, face),
        in_specs=[SMEM, VMEM, ANY, ANY, VMEM],
        out_specs=(VMEM, VMEM, VMEM),
        scratch_shapes=[
            pltpu.VMEM((4, NF, NF, layers, cells), jnp.float32),
            pltpu.VMEM((3, NF, NF, layers, cells), jnp.float32),
            pltpu.VMEM((NF, 8, cells), jnp.float32),
            pltpu.VMEM((NF, 8, cells), jnp.float32),
            pltpu.SemaphoreType.DMA((7,)),
        ],
        cost_estimate=pl.CostEstimate(flops=350 * layers * cells, bytes_accessed=3_000_000, transcendentals=0),
        compiler_params=pltpu.CompilerParams(vmem_limit_bytes=16 * 2**20),
        name="stencil",
    )(space_at, own, jac_x[0], jac_local[0], objective_gradient[0])
    near = lax.ppermute(near, "space", [(i, i ^ 1) for i in range(count)])
    far = lax.ppermute(far, "space", [pair for i in range(1, count - 1, 2) for pair in ((i, i + 1), (i + 1, i))])
    table = spectral_table(NT)
    mine = np.stack([table[i, i % 2::2] for i in range(NT)])
    theirs = np.stack([table[i ^ 1, i % 2::2] for i in range(NT)])
    coefficients = lax.dynamic_index_in_dim(jnp.asarray(np.stack([mine, theirs], 1)), here, 0, keepdims=False)
    combined = pl.pallas_call(
        combine_kernel,
        out_shape=jax.ShapeDtypeStruct((PAIRS, NF, layers, cells), jnp.float32),
        in_specs=[SMEM, VMEM, VMEM],
        out_specs=VMEM,
        cost_estimate=pl.CostEstimate(flops=12 * NF * layers * cells, bytes_accessed=500_000, transcendentals=0),
        name="combine",
    )(coefficients, own, other)
    groups = [list(range(parity, NT, 2)) for parity in range(2)]
    spectral = lax.all_to_all(combined, "tm", 0, 0, tiled=True, axis_index_groups=groups)
    out = pl.pallas_call(
        finish_kernel,
        out_shape=field,
        in_specs=[SMEM, VMEM, VMEM, VMEM, VMEM, VMEM, VMEM, VMEM],
        out_specs=VMEM,
        scratch_shapes=[
            pltpu.VMEM(((NF + 1) // 2, 8, cells), jnp.float32),
            pltpu.VMEM(((NF + 1) // 2, 8, cells), jnp.float32),
        ],
        cost_estimate=pl.CostEstimate(flops=30 * NF * layers * cells, bytes_accessed=800_000, transcendentals=0),
        name="finish",
    )(space_at, part, spectral, volume, near, far, face_lower, face_upper)
    return out[None]


def solution(mesh):
    in_specs = (
        P("tm", None, "space", None),
        P("tm", None, None, None, "space", None),
        P("tm", None, None, None, "space", None),
        P("tm", None, "space", None),
        P("space", None),
        P("space", None),
        P("space", None),
    )
    out_specs = P("tm", None, "space", None)
    return jax.shard_map(body, mesh=mesh, in_specs=in_specs, out_specs=out_specs, check_vma=False)
```

time: 115 us -> 41.6 us (0.36)
  the two profiles are of different devices: /device:TPU:392 before, /device:TPU:251 now
where the time goes in v1:
time: 41.6 us; the launch traced here: 41.2 us
  starting transfers between devices  19.5 us (47%)
  waiting for transfers between devices  8.14 us (20%)
  local copies, waits for them, and re-layouts  7.7 us (19%)
  Pallas kernels  5.79 us (14%)
    ppermute x1, starting transfers between devices, body(): lax.ppermute(far, 'space', [pair for i in range(1, count - 1, 2) for pair...  7.62 us
    unnamed x18, local copies, waits for them, and re-layouts  6.47 us
    ppermute x1, waiting for transfers between devices, body(): other = lax.ppermute(own, 'tm', [(i, i ^ 1) for i in range(NT)])  6.24 us
    ppermute x1, starting transfers between devices, body(): other = lax.ppermute(own, 'tm', [(i, i ^ 1) for i in range(NT)])  4.42 us
    all_to_all x1, starting transfers between devices, body(): lax.all_to_all(combined, 'tm', 0, 0, tiled=True, axis_index_groups=groups)  4.26 us
    ppermute x1, starting transfers between devices, body(): near = lax.ppermute(near, 'space', [(i, i ^ 1) for i in range(count)])  3.17 us
    pallas_call x1, Pallas kernels, body(): pl.pallas_call(stencil_kernel, out_shape=(field, face, face), in_specs=[S...  2.09 us
    pallas_call x1, Pallas kernels, body(): pl.pallas_call(finish_kernel, out_shape=field, in_specs=[SMEM, VMEM, VMEM...  2 us
  transfers between devices with their start and end apart: 4, of which 2 were waited for; matrix products, arithmetic and copies ran while one was open for 3% of the time, Pallas kernels for 5%

profile of v1, /device:TPU:251, one launch (start us, length us, event | category | flops | bytes accessed | tf_op | source)
XLA Modules:
  0.0 41.2 jit_solution(2848245592006023923)
XLA Ops:
  0.0 4.4 %collective-permute-start = (f32[5,4,1024]{2,1,0:T(4,128)}, f32[5,4,1024]{2,1,0:T(4,128)S(1)}, u32[]{:S(2)}, u32[]{:S(2)}) collective-permute-start(f32[5,4,1024]{2,1,0:T(4,128)} %bitcast.10), channel_id=1, source_target_pairs={{0,64},{64,0},{128,192},{192,128},{256,320},{320,256},{384,448},{4... | collective-permute-start | bytes 245768 | tf_op jit(solution)/shard_map/ppermute | solution.py:116
  4.4 1.2 %dynamic-slice_bitcast_fusion.coef_ref = f32[2,4]{1,0:T(2,128)} fusion(f32[8,2,4]{2,1,0:T(2,128)} %constant.17.clone, s32[]{:T(128)S(6)} %select_n.4), kind=kLoop, calls=%fused_computation | loop fusion | bytes 68 | tf_op jit(solution)/shard_map/jit(dynamic_index_in_dim)/squeeze | solution.py:139
  5.7 6.2 %collective-permute-done.other_ref = f32[5,4,1024]{2,1,0:T(4,128)S(1)} collective-permute-done((f32[5,4,1024]{2,1,0:T(4,128)}, f32[5,4,1024]{2,1,0:T(4,128)S(1)}, u32[]{:S(2)}, u32[]{:S(2)}) %collective-permute-start) | collective-permute-done | bytes 81952 | tf_op jit(solution)/shard_map/ppermute | solution.py:116
  11.9 0.0 copy-start.6
  11.9 0.6 %copy-done.6 = f32[5,4,1024]{2,1,0:T(4,128)} copy-done((f32[5,4,1024]{2,1,0:T(4,128)}, f32[5,4,1024]{2,1,0:T(4,128)S(1)}, u32[]{:S(2)}) %copy-start.6) | copy-done | bytes 81944
  12.5 1.7 %combine.1 = f32[4,5,4,1024]{3,2,1,0:T(4,128)} custom-call(f32[2,4]{1,0:T(2,128)} %dynamic-slice_bitcast_fusion.coef_ref, f32[5,4,1024]{2,1,0:T(4,128)} %bitcast.11, f32[5,4,1024]{2,1,0:T(4,128)} %copy-done.6), custom_call_target="tpu_custom_call" | custom-call | flops 245760 | bytes 500000 | tf_op jit(solution)/shard_map/combine/pallas_call | solution.py:140
  14.2 4.3 %all-to-all-start = ((f32[4,5,4,1024]{3,2,1,0:T(4,128)}), f32[4,5,4,1024]{3,2,1,0:T(4,128)S(1)}, u32[]{:S(2)}, u32[]{:S(2)}) async-start(f32[4,5,4,1024]{3,2,1,0:T(4,128)} %combine.1), calls=%async_computation | async-start | bytes 655360 | tf_op jit(solution)/shard_map/all_to_all | solution.py:149
  18.5 0.0 copy-start
  18.5 1.4 %copy-done = f32[1,4,5,5,4,1024]{5,4,3,2,1,0:T(4,128)S(1)} copy-done((f32[1,4,5,5,4,1024]{5,4,3,2,1,0:T(4,128)S(1)}, f32[1,4,5,5,4,1024]{5,4,3,2,1,0:T(4,128)}, u32[]{:S(2)}) %copy-start) | copy-done | bytes 1638424
  19.9 0.0 copy-start.1
  19.9 1.3 %copy-done.1 = f32[1,3,5,5,4,1024]{5,4,3,2,1,0:T(4,128)S(1)} copy-done((f32[1,3,5,5,4,1024]{5,4,3,2,1,0:T(4,128)S(1)}, f32[1,3,5,5,4,1024]{5,4,3,2,1,0:T(4,128)}, u32[]{:S(2)}) %copy-start.1) | copy-done | bytes 1228824
  21.2 0.0 copy-start.2
  21.2 0.9 %copy-done.2 = f32[1,5,4,1024]{3,2,1,0:T(4,128)S(1)} copy-done((f32[1,5,4,1024]{3,2,1,0:T(4,128)S(1)}, f32[1,5,4,1024]{3,2,1,0:T(4,128)}, u32[]{:S(2)}) %copy-start.2) | copy-done | bytes 81944
  22.1 0.0 copy-start.3
  22.1 0.9 %copy-done.3 = f32[1,5,4,1024]{3,2,1,0:T(4,128)S(1)} copy-done((f32[1,5,4,1024]{3,2,1,0:T(4,128)S(1)}, f32[1,5,4,1024]{3,2,1,0:T(4,128)}, u32[]{:S(2)}) %copy-start.3) | copy-done | bytes 81944
  23.0 2.1 %stencil.1 = (f32[5,4,1024]{2,1,0:T(4,128)S(1)}, f32[5,2,1024]{2,1,0:T(2,128)S(1)}, f32[5,2,1024]{2,1,0:T(2,128)S(1)}) custom-call(s32[1]{0:T(128)} %bitcast.space_ref, f32[5,4,1024]{2,1,0:T(4,128)S(1)} %bitcast.12, f32[4,5,5,4,1024]{4,3,2,1,0:T(4,128)S(1)} %bitcast.8, f32[3,5,5,4,1024]{4,3,2,1,0:T(4,128)S(1)} %bitcast.9, f32[5,4,1024]{2,1,0:T(4,128)S(1)} %bitcast.13), custom_call_target="tpu_custom_call" | custom-call | flops 1433600 | bytes 3000000 | tf_op jit(solution)/shard_map/stencil/pallas_call | solution.py:118
  25.1 0.0 copy-start.4
  25.1 0.6 %copy-done.4 = f32[5,4,1024]{2,1,0:T(4,128)} copy-done((f32[5,4,1024]{2,1,0:T(4,128)}, f32[5,4,1024]{2,1,0:T(4,128)S(1)}, u32[]{:S(2)}) %copy-start.4) | copy-done | bytes 81944
  25.7 3.2 %collective-permute-start.1 = (f32[5,2,1024]{2,1,0:T(2,128)S(1)}, f32[5,2,1024]{2,1,0:T(2,128)S(1)}, u32[]{:S(2)}, u32[]{:S(2)}) collective-permute-start(f32[5,2,1024]{2,1,0:T(2,128)S(1)} %get-tuple-element.9), channel_id=1, source_target_pairs={{0,1},{1,0},{2,3},{3,2},{4,5},{5,4},{6,7},{7,6},{8,9},{9,8},{10,11... | collective-permute-start | bytes 122888 | tf_op jit(solution)/shard_map/ppermute | solution.py:134
  28.9 7.6 %collective-permute-start.2 = (f32[5,2,1024]{2,1,0:T(2,128)S(1)}, f32[5,2,1024]{2,1,0:T(2,128)S(1)}, u32[]{:S(2)}, u32[]{:S(2)}) collective-permute-start(f32[5,2,1024]{2,1,0:T(2,128)S(1)} %get-tuple-element.10), channel_id=1, source_target_pairs={{1,2},{2,1},{3,4},{4,3},{5,6},{6,5},{7,8},{8,7},{9,10},{10,9},{11,... | collective-permute-start | bytes 122888 | tf_op jit(solution)/shard_map/ppermute | solution.py:135
  36.5 0.0 collective-permute-done.1.near_ref
  36.5 0.0 copy-start.7
  36.5 1.9 %collective-permute-done.2.far_ref = f32[5,2,1024]{2,1,0:T(2,128)S(1)} collective-permute-done((f32[5,2,1024]{2,1,0:T(2,128)S(1)}, f32[5,2,1024]{2,1,0:T(2,128)S(1)}, u32[]{:S(2)}, u32[]{:S(2)}) %collective-permute-start.2) | collective-permute-done | bytes 40992 | tf_op jit(solution)/shard_map/ppermute | solution.py:135
  38.4 0.0 copy-start.8
  38.4 0.0 all-to-all-done.spec_ref
  38.4 0.0 copy-start.5
  38.4 0.0 copy-done.7
  38.5 0.6 %copy-done.8 = f32[5,2,1024]{2,1,0:T(2,128)} copy-done((f32[5,2,1024]{2,1,0:T(2,128)}, f32[5,2,1024]{2,1,0:T(2,128)S(1)}, u32[]{:S(2)}) %copy-start.8) | copy-done | bytes 40984
  39.1 0.1 copy-done.5
  39.2 2.0 %finish.1 = f32[5,4,1024]{2,1,0:T(4,128)} custom-call(s32[1]{0:T(128)} %bitcast.space_ref, f32[5,4,1024]{2,1,0:T(4,128)} %copy-done.4, f32[4,5,4,1024]{3,2,1,0:T(4,128)} %copy-done.5, f32[4,1024]{1,0:T(4,128)} %vol_ref.1, f32[5,2,1024]{2,1,0:T(2,128)} %copy-done.7, f32[5,2,1024]{2,1,0:T(2,128)} %copy-done.8, s32[1,1024]{1,0:T(1,128)} %low_ref.1, ...), custom_call_target="tpu_custom_call" | custom-call | flops 614400 | bytes 800000 | tf_op jit(solution)/shard_map/finish/pallas_call | solution.py:150
Async XLA Ops:
  0.0 11.9 %collective-permute-start = (f32[5,4,1024]{2,1,0:T(4,128)}, f32[5,4,1024]{2,1,0:T(4,128)S(1)}, u32[]{:S(2)}, u32[]{:S(2)}) collective-permute-start(f32[5,4,1024]{2,1,0:T(4,128)} %bitcast.10), channel_id=1, source_target_pairs={{0,64},{64,0},{128,192},{192,128},{256,320},{320,256},{384,448},{4... | collective-permute-start | bytes 245768 | tf_op jit(solution)/shard_map/ppermute | solution.py:116
  11.9 0.6 %copy-start.6 = (f32[5,4,1024]{2,1,0:T(4,128)}, f32[5,4,1024]{2,1,0:T(4,128)S(1)}, u32[]{:S(2)}) copy-start(f32[5,4,1024]{2,1,0:T(4,128)S(1)} %collective-permute-done.other_ref) | copy-start | bytes 245764
  14.2 24.2 %all-to-all-start = ((f32[4,5,4,1024]{3,2,1,0:T(4,128)}), f32[4,5,4,1024]{3,2,1,0:T(4,128)S(1)}, u32[]{:S(2)}, u32[]{:S(2)}) async-start(f32[4,5,4,1024]{3,2,1,0:T(4,128)} %combine.1), calls=%async_computation | async-start | bytes 655360 | tf_op jit(solution)/shard_map/all_to_all | solution.py:149
  18.5 1.4 %copy-start = (f32[1,4,5,5,4,1024]{5,4,3,2,1,0:T(4,128)S(1)}, f32[1,4,5,5,4,1024]{5,4,3,2,1,0:T(4,128)}, u32[]{:S(2)}) copy-start(f32[1,4,5,5,4,1024]{5,4,3,2,1,0:T(4,128)} %param.9) | copy-start | bytes 4915204
  19.9 1.3 %copy-start.1 = (f32[1,3,5,5,4,1024]{5,4,3,2,1,0:T(4,128)S(1)}, f32[1,3,5,5,4,1024]{5,4,3,2,1,0:T(4,128)}, u32[]{:S(2)}) copy-start(f32[1,3,5,5,4,1024]{5,4,3,2,1,0:T(4,128)} %param.10) | copy-start | bytes 3686404
  21.2 0.9 %copy-start.2 = (f32[1,5,4,1024]{3,2,1,0:T(4,128)S(1)}, f32[1,5,4,1024]{3,2,1,0:T(4,128)}, u32[]{:S(2)}) copy-start(f32[1,5,4,1024]{3,2,1,0:T(4,128)} %param.8) | copy-start | bytes 245764
  22.1 0.9 %copy-start.3 = (f32[1,5,4,1024]{3,2,1,0:T(4,128)S(1)}, f32[1,5,4,1024]{3,2,1,0:T(4,128)}, u32[]{:S(2)}) copy-start(f32[1,5,4,1024]{3,2,1,0:T(4,128)} %param.11) | copy-start | bytes 245764
  25.1 0.6 %copy-start.4 = (f32[5,4,1024]{2,1,0:T(4,128)}, f32[5,4,1024]{2,1,0:T(4,128)S(1)}, u32[]{:S(2)}) copy-start(f32[5,4,1024]{2,1,0:T(4,128)S(1)} %get-tuple-element.8.part_ref) | copy-start | bytes 245764
  25.7 10.8 %collective-permute-start.1 = (f32[5,2,1024]{2,1,0:T(2,128)S(1)}, f32[5,2,1024]{2,1,0:T(2,128)S(1)}, u32[]{:S(2)}, u32[]{:S(2)}) collective-permute-start(f32[5,2,1024]{2,1,0:T(2,128)S(1)} %get-tuple-element.9), channel_id=1, source_target_pairs={{0,1},{1,0},{2,3},{3,2},{4,5},{5,4},{6,7},{7,6},{8,9},{9,8},{10,11... | collective-permute-start | bytes 122888 | tf_op jit(solution)/shard_map/ppermute | solution.py:134
  28.9 9.5 %collective-permute-start.2 = (f32[5,2,1024]{2,1,0:T(2,128)S(1)}, f32[5,2,1024]{2,1,0:T(2,128)S(1)}, u32[]{:S(2)}, u32[]{:S(2)}) collective-permute-start(f32[5,2,1024]{2,1,0:T(2,128)S(1)} %get-tuple-element.10), channel_id=1, source_target_pairs={{1,2},{2,1},{3,4},{4,3},{5,6},{6,5},{7,8},{8,7},{9,10},{10,9},{11,... | collective-permute-start | bytes 122888 | tf_op jit(solution)/shard_map/ppermute | solution.py:135
  36.5 1.9 %copy-start.7 = (f32[5,2,1024]{2,1,0:T(2,128)}, f32[5,2,1024]{2,1,0:T(2,128)S(1)}, u32[]{:S(2)}) copy-start(f32[5,2,1024]{2,1,0:T(2,128)S(1)} %collective-permute-done.1.near_ref) | copy-start | bytes 122884
  38.4 0.6 %copy-start.8 = (f32[5,2,1024]{2,1,0:T(2,128)}, f32[5,2,1024]{2,1,0:T(2,128)S(1)}, u32[]{:S(2)}) copy-start(f32[5,2,1024]{2,1,0:T(2,128)S(1)} %collective-permute-done.2.far_ref) | copy-start | bytes 122884
  38.4 0.7 %copy-start.5 = (f32[4,5,4,1024]{3,2,1,0:T(4,128)}, f32[4,5,4,1024]{3,2,1,0:T(4,128)S(1)}, u32[]{:S(2)}) copy-start(f32[4,5,4,1024]{3,2,1,0:T(4,128)S(1)} %all-to-all-done.spec_ref) | copy-start | bytes 983044

commit v2 on v1

v2 whole, which is shorter than its diff:
```python
import jax
import jax.numpy as jnp
import numpy as np
from jax import lax
from jax.experimental import pallas as pl
from jax.experimental.pallas import tpu as pltpu
from jax.sharding import PartitionSpec as P

NT = 8
NF = 5
PAIRS = NT // 2
VMEM = pl.BlockSpec(memory_space=pltpu.VMEM)
HBM = pl.BlockSpec(memory_space=pltpu.HBM)


def spectral_table(count):
    index = np.arange(count)
    offset = index[:, None] - index[None, :]
    parity = np.where(offset % 2 == 0, 1.0, -1.0)
    mask = np.logical_and(offset != 0, np.abs(offset) * 2 != count)
    safe = np.where(mask, offset, 1)
    first = np.where(mask, 0.5 * parity / np.tan(np.pi * safe / count), 0.0)
    apart = offset != 0
    wide = np.where(apart, offset, 1)
    sine = np.sin(np.pi * wide / count)
    second = np.where(apart, -0.5 * parity / (sine * sine), -(count * count + 2) / 12.0)
    return (first + 0.25 * second).astype(np.float32)


def products(fields, blocks, k, b, here):
    total = blocks[k, 0, b, :, here] * fields[0]
    for a in range(1, NF):
        total = total + blocks[k, a, b, :, here] * fields[a]
    return total


def across_kernel(adj_hbm, jac_hbm, own_ref, inner_ref, near_ref, far_ref, jac, ext, sems):
    first = pltpu.make_async_copy(adj_hbm, own_ref, sems.at[0])
    first.start()
    copies = [pltpu.make_async_copy(jac_hbm.at[k], jac.at[k], sems.at[1 + k]) for k in range(4)]
    for copy in copies:
        copy.start()
    cells = own_ref.shape[2]
    ext[...] = jnp.zeros_like(ext)
    first.wait()
    for k, offset in enumerate((1, -1, 2, -2)):
        copies[k].wait()
        for at in range(0, cells, 128):
            here = slice(at, at + 128)
            fields = [own_ref[a, :, here] for a in range(NF)]
            for b in range(NF):
                ext[b, 2 + offset:6 + offset, here] += products(fields, jac, k, b, here)
    even = lax.axis_index("space") % 2 == 0
    for b in range(NF):
        below = ext[b, 0:2, :]
        above = ext[b, 6:8, :]
        inner_ref[b] = ext[b, 2:6, :]
        near_ref[b] = jnp.where(even, above, below)
        far_ref[b] = jnp.where(even, below, above)


def along_kernel(own_ref, inner_ref, jac_hbm, obj_hbm, part_ref, jac, obj, side, sems):
    copies = [pltpu.make_async_copy(jac_hbm.at[k], jac.at[k], sems.at[k]) for k in range(3)]
    last = pltpu.make_async_copy(obj_hbm, obj, sems.at[3])
    for copy in copies[1:]:
        copy.start()
    copies[0].start()
    last.start()
    cells = own_ref.shape[2]
    side[...] = jnp.zeros_like(side)
    lane = lax.broadcasted_iota(jnp.int32, (8, cells), 1)
    for k in (1, 2, 0):
        copies[k].wait()
        for at in range(0, cells, 128):
            here = slice(at, at + 128)
            fields = [own_ref[a, :, here] for a in range(NF)]
            for b in range(NF):
                total = products(fields, jac, k, b, here)
                if k == 0:
                    part_ref[b, :, here] = total
                else:
                    side[k - 1, b, 0:4, here] = total
    last.wait()
    for b in range(NF):
        plus = jnp.where(lane == 0, 0.0, pltpu.roll(side[0, b], 1, 1))
        minus = jnp.where(lane == cells - 1, 0.0, pltpu.roll(side[1, b], cells - 1, 1))
        side[0, b] = plus + minus
        part_ref[b] = part_ref[b] + obj[b] + inner_ref[b] + side[0, b, 0:4, :]


def combine_kernel(own_ref, other_ref, out_ref):
    at = lax.axis_index("tm")
    odd = at % 2 == 1
    table = spectral_table(NT)
    for j in range(PAIRS):
        ours = float(table[0, 2 * j])
        theirs = jnp.where(odd, float(table[0, (2 * j + 1) % NT]), float(table[1, 2 * j]))
        out_ref[(at // 2 + j) % PAIRS] = ours * own_ref[...] + theirs * other_ref[...]


def faces_kernel(part_ref, near_ref, far_ref, low_ref, up_ref, out_ref, halo, moved):
    odd = lax.axis_index("space") % 2 == 1
    cells = low_ref.shape[1]
    halo[...] = jnp.zeros_like(halo)
    for b in range(NF):
        row = 4 * (b % 2)
        halo[b // 2, row:row + 2, :] = jnp.where(odd, near_ref[b], far_ref[b])
        halo[b // 2, row + 2:row + 4, :] = jnp.where(odd, far_ref[b], near_ref[b])
    groups = halo.shape[0]
    chunks = cells // 128
    from_low = lax.broadcasted_iota(jnp.int32, (8, 128), 0) % 4 < 2
    for j in range(chunks):
        here = slice(128 * j, 128 * (j + 1))
        low = jnp.broadcast_to(low_ref[0:1, here], (8, 128))
        up = jnp.broadcast_to(up_ref[0:1, here], (8, 128))
        index = jnp.where(from_low, low, up)
        lane = index % 128
        chunk = index // 128
        for g in range(groups):
            total = None
            for c in range(chunks):
                piece = jnp.take_along_axis(halo[g, :, 128 * c:128 * (c + 1)], lane, axis=1, mode="promise_in_bounds")
                total = piece if c == 0 else jnp.where(chunk == c, piece, total)
            moved[g, :, here] = total
    for b in range(NF):
        row = 4 * (b % 2)
        out_ref[b] = part_ref[b] + moved[b // 2, row:row + 4, :]


def finish_kernel(part_ref, spec_ref, vol_ref, out_ref):
    scale = 1.5 * vol_ref[...]
    for b in range(NF):
        spectral = spec_ref[0, b]
        for j in range(1, PAIRS):
            spectral = spectral + spec_ref[j, b]
        out_ref[b] = part_ref[b] + scale * spectral


def kernel_call(kernel, name, out_shape, in_specs, scratch=(), out_specs=None, limit=2**20, flops=0, moved=0):
    if out_specs is None:
        out_specs = jax.tree.map(lambda _: VMEM, out_shape)
    return pl.pallas_call(
        kernel,
        out_shape=out_shape,
        in_specs=in_specs,
        out_specs=out_specs,
        scratch_shapes=scratch,
        cost_estimate=pl.CostEstimate(flops=flops, bytes_accessed=moved, transcendentals=0),
        compiler_params=pltpu.CompilerParams(vmem_limit_bytes=limit),
        name=name,
    )


def body(adjoint, jac_x, jac_local, objective_gradient, volume, face_lower, face_upper):
    _, _, layers, cells = adjoint.shape
    count = lax.axis_size("space")
    block = NF * layers * cells
    field = jax.ShapeDtypeStruct((NF, layers, cells), jnp.float32)
    face = jax.ShapeDtypeStruct((NF, 2, cells), jnp.float32)
    other = lax.ppermute(adjoint[0], "tm", [(i, i ^ 1) for i in range(NT)])
    own, inner, near, far = kernel_call(
        across_kernel, "across", (field, field, face, face), [HBM, HBM],
        [
            pltpu.VMEM((4, NF, NF, layers, cells), jnp.float32),
            pltpu.VMEM((NF, 8, cells), jnp.float32),
            pltpu.SemaphoreType.DMA((5,)),
        ],
        limit=3 * 2**20, flops=40 * block, moved=84 * block,
    )(adjoint[0], jac_x[0])
    far = lax.ppermute(far, "space", [pair for i in range(1, count - 1, 2) for pair in ((i, i + 1), (i + 1, i))])
    combined = kernel_call(
        combine_kernel, "combine", jax.ShapeDtypeStruct((PAIRS, NF, layers, cells), jnp.float32), [VMEM, VMEM],
        flops=12 * block, moved=24 * block,
    )(own, other)
    groups = [list(range(parity, NT, 2)) for parity in range(2)]
    spectral = lax.all_to_all(combined, "tm", 0, 0, tiled=True, axis_index_groups=groups)
    near = lax.ppermute(near, "space", [(i, i ^ 1) for i in range(count)])
    part = kernel_call(
        along_kernel, "along", field, [VMEM, VMEM, HBM, HBM],
        [
            pltpu.VMEM((3, NF, NF, layers, cells), jnp.float32),
            pltpu.VMEM((NF, layers, cells), jnp.float32),
            pltpu.VMEM((2, NF, 8, cells), jnp.float32),
            pltpu.SemaphoreType.DMA((4,)),
        ],
        limit=3 * 2**20, flops=30 * block, moved=80 * block,
    )(own, inner, jac_local[0], objective_gradient[0])
    part = kernel_call(
        faces_kernel, "faces", field, [VMEM] * 5,
        [
            pltpu.VMEM(((NF + 1) // 2, 8, cells), jnp.float32),
            pltpu.VMEM(((NF + 1) // 2, 8, cells), jnp.float32),
        ],
        flops=20 * block, moved=20 * block,
    )(part, near, far, face_lower, face_upper)
    out = kernel_call(
        finish_kernel, "finish", field, [VMEM] * 3, flops=5 * block, moved=24 * block,
    )(part, spectral, volume)
    return out[None]


def solution(mesh):
    in_specs = (
        P("tm", None, "space", None),
        P("tm", None, None, None, "space", None),
        P("tm", None, None, None, "space", None),
        P("tm", None, "space", None),
        P("space", None),
        P("space", None),
        P("space", None),
    )
    out_specs = P("tm", None, "space", None)
    return jax.shard_map(body, mesh=mesh, in_specs=in_specs, out_specs=out_specs, check_vma=False)
```

time: 41.6 us -> 31 us (0.75)
  local copies, waits for them, and re-layouts: 7.7 us -> 2.34 us
  waiting for transfers between devices: 8.14 us -> 4.48 us
  Pallas kernels: 5.79 us -> 4.3 us
    unnamed x18 -> x14, local copies, waits for them, and re-layouts: 6.47 us -> 2.34 us
    ppermute x1, waiting for transfers between devices: 6.24 us -> 3.77 us  [body(): other = lax.ppermute(adjoint[0], 'tm', [(i, i ^ 1) for i in range(NT)])]
    pallas_call x3 -> x5, Pallas kernels: 5.79 us -> 4.3 us  [the longest x1 1.34 us: body(): kernel_call(across_kernel, 'across', (field, field, face, face), [HBM, HB...]
    squeeze x1 -> x0, local copies, waits for them, and re-layouts: 1.23 us -> none  [body(): lax.dynamic_index_in_dim(jnp.asarray(np.stack([mine, theirs], 1)), here,...]
    ppermute x1, waiting for transfers between devices: 1.9 us -> 0.71 us  [body(): lax.ppermute(far, 'space', [pair for i in range(1, count - 1, 2) for pair...]
  transfers between devices with their start and end apart: 4 -> 4, of which waited for: 2 -> 2; matrix products, arithmetic and copies ran while one was open for 3% -> 0% of each run, Pallas kernels for 5% -> 9%
where the time goes in v2:
time: 31 us; the launch traced here: 30.7 us
  starting transfers between devices  19.5 us (63%)
  waiting for transfers between devices  4.48 us (14%)
  Pallas kernels  4.3 us (14%)
  local copies, waits for them, and re-layouts  2.34 us (8%)
    ppermute x1, starting transfers between devices, body(): lax.ppermute(far, 'space', [pair for i in range(1, count - 1, 2) for pair...  7.62 us
    ppermute x1, starting transfers between devices, body(): other = lax.ppermute(adjoint[0], 'tm', [(i, i ^ 1) for i in range(NT)])  4.42 us
    all_to_all x1, starting transfers between devices, body(): lax.all_to_all(combined, 'tm', 0, 0, tiled=True, axis_index_groups=groups)  4.26 us
    ppermute x1, waiting for transfers between devices, body(): other = lax.ppermute(adjoint[0], 'tm', [(i, i ^ 1) for i in range(NT)])  3.77 us
    ppermute x1, starting transfers between devices, body(): near = lax.ppermute(near, 'space', [(i, i ^ 1) for i in range(count)])  3.17 us
    unnamed x14, local copies, waits for them, and re-layouts  2.34 us
    pallas_call x1, Pallas kernels, body(): kernel_call(across_kernel, 'across', (field, field, face, face), [HBM, HB...  1.34 us
    pallas_call x1, Pallas kernels, body(): kernel_call(along_kernel, 'along', field, [VMEM, VMEM, HBM, HBM], [pltpu....  1.17 us
  transfers between devices with their start and end apart: 4, of which 2 were waited for; matrix products, arithmetic and copies ran while one was open for 0% of the time, Pallas kernels for 9%

profile of v2, /device:TPU:251, one launch (start us, length us, event | category | flops | bytes accessed | tf_op | source)
XLA Modules:
  0.0 30.7 jit_solution(4934168559853550830)
XLA Ops:
  0.0 4.4 %collective-permute-start.2 = (f32[5,4,1024]{2,1,0:T(4,128)}, f32[5,4,1024]{2,1,0:T(4,128)S(1)}, u32[]{:S(2)}, u32[]{:S(2)}) collective-permute-start(f32[5,4,1024]{2,1,0:T(4,128)} %bitcast.8), channel_id=1, source_target_pairs={{0,64},{64,0},{128,192},{192,128},{256,320},{320,256},{384,448},{4... | collective-permute-start | bytes 245768 | tf_op jit(solution)/shard_map/ppermute | solution.py:160
  4.4 0.0 copy-start
  4.4 1.4 %copy-done = f32[1,4,5,5,4,1024]{5,4,3,2,1,0:T(4,128)S(1)} copy-done((f32[1,4,5,5,4,1024]{5,4,3,2,1,0:T(4,128)S(1)}, f32[1,4,5,5,4,1024]{5,4,3,2,1,0:T(4,128)}, u32[]{:S(2)}) %copy-start) | copy-done | bytes 1638424
  5.9 0.0 copy-start.3
  5.9 0.9 %copy-done.3 = f32[1,5,4,1024]{3,2,1,0:T(4,128)S(1)} copy-done((f32[1,5,4,1024]{3,2,1,0:T(4,128)S(1)}, f32[1,5,4,1024]{3,2,1,0:T(4,128)}, u32[]{:S(2)}) %copy-start.3) | copy-done | bytes 81944
  6.7 0.0 copy-start.1
  6.8 0.0 copy-start.2
  6.8 1.3 %across.1 = (f32[5,4,1024]{2,1,0:T(4,128)S(1)}, f32[5,4,1024]{2,1,0:T(4,128)S(1)}, f32[5,2,1024]{2,1,0:T(2,128)S(1)}, f32[5,2,1024]{2,1,0:T(2,128)S(1)}) custom-call(f32[5,4,1024]{2,1,0:T(4,128)S(1)} %bitcast.9, f32[4,5,5,4,1024]{4,3,2,1,0:T(4,128)S(1)} %bitcast.5), custom_call_target="tpu_custom_call" | custom-call | flops 819200 | bytes 1720320 | tf_op jit(solution)/shard_map/across/pallas_call | solution.py:161
  8.1 0.0 copy-start.5
  8.1 0.0 copy-start.6
  8.1 0.0 copy-start.4
  8.1 3.8 %collective-permute-done.2.other_ref = f32[5,4,1024]{2,1,0:T(4,128)S(1)} collective-permute-done((f32[5,4,1024]{2,1,0:T(4,128)}, f32[5,4,1024]{2,1,0:T(4,128)S(1)}, u32[]{:S(2)}, u32[]{:S(2)}) %collective-permute-start.2) | collective-permute-done | bytes 81952 | tf_op jit(solution)/shard_map/ppermute | solution.py:160
  11.9 0.8 %combine.1 = f32[4,5,4,1024]{3,2,1,0:T(4,128)} custom-call(f32[5,4,1024]{2,1,0:T(4,128)S(1)} %get-tuple-element.9.own_ref, f32[5,4,1024]{2,1,0:T(4,128)S(1)} %collective-permute-done.2.other_ref), custom_call_target="tpu_custom_call" | custom-call | flops 245760 | bytes 491520 | tf_op jit(solution)/shard_map/combine/pallas_call | solution.py:171
  12.7 4.3 %all-to-all-start = ((f32[4,5,4,1024]{3,2,1,0:T(4,128)}), f32[4,5,4,1024]{3,2,1,0:T(4,128)S(1)}, u32[]{:S(2)}, u32[]{:S(2)}) async-start(f32[4,5,4,1024]{3,2,1,0:T(4,128)} %combine.1), calls=%async_computation | async-start | bytes 655360 | tf_op jit(solution)/shard_map/all_to_all | solution.py:176
  16.9 3.2 %collective-permute-start = (f32[5,2,1024]{2,1,0:T(2,128)S(1)}, f32[5,2,1024]{2,1,0:T(2,128)S(1)}, u32[]{:S(2)}, u32[]{:S(2)}) collective-permute-start(f32[5,2,1024]{2,1,0:T(2,128)S(1)} %get-tuple-element.11), channel_id=1, source_target_pairs={{0,1},{1,0},{2,3},{3,2},{4,5},{5,4},{6,7},{7,6},{8,9},{9,8},{10,11... | collective-permute-start | bytes 122888 | tf_op jit(solution)/shard_map/ppermute | solution.py:177
  20.1 7.6 %collective-permute-start.1 = (f32[5,2,1024]{2,1,0:T(2,128)S(1)}, f32[5,2,1024]{2,1,0:T(2,128)S(1)}, u32[]{:S(2)}, u32[]{:S(2)}) collective-permute-start(f32[5,2,1024]{2,1,0:T(2,128)S(1)} %get-tuple-element.12), channel_id=1, source_target_pairs={{1,2},{2,1},{3,4},{4,3},{5,6},{6,5},{7,8},{8,7},{9,10},{10,9},{11,... | collective-permute-start | bytes 122888 | tf_op jit(solution)/shard_map/ppermute | solution.py:170
  27.8 0.0 copy-done.1
  27.8 0.0 copy-done.2
  27.8 1.2 %along.1.part_ref = f32[5,4,1024]{2,1,0:T(4,128)S(1)} custom-call(f32[5,4,1024]{2,1,0:T(4,128)S(1)} %get-tuple-element.9.own_ref, f32[5,4,1024]{2,1,0:T(4,128)S(1)} %get-tuple-element.10.inner_ref, f32[3,5,5,4,1024]{4,3,2,1,0:T(4,128)S(1)} %bitcast.6, f32[5,4,1024]{2,1,0:T(4,128)S(1)} %bitcast.7), custom_call_target="tpu_custom_call" | custom-call | flops 614400 | bytes 1638400 | tf_op jit(solution)/shard_map/along/pallas_call | solution.py:178
  29.0 0.0 collective-permute-done.near_ref
  29.0 0.7 %collective-permute-done.1.far_ref = f32[5,2,1024]{2,1,0:T(2,128)S(1)} collective-permute-done((f32[5,2,1024]{2,1,0:T(2,128)S(1)}, f32[5,2,1024]{2,1,0:T(2,128)S(1)}, u32[]{:S(2)}, u32[]{:S(2)}) %collective-permute-start.1) | collective-permute-done | bytes 40992 | tf_op jit(solution)/shard_map/ppermute | solution.py:170
  29.7 0.0 copy-done.5
  29.7 0.0 copy-done.6
  29.7 0.3 %faces.1.part_ref = f32[5,4,1024]{2,1,0:T(4,128)S(1)} custom-call(f32[5,4,1024]{2,1,0:T(4,128)S(1)} %along.1.part_ref, f32[5,2,1024]{2,1,0:T(2,128)S(1)} %collective-permute-done.near_ref, f32[5,2,1024]{2,1,0:T(2,128)S(1)} %collective-permute-done.1.far_ref, s32[1,1024]{1,0:T(1,128)S(1)} %copy-done.5, s32[1,1024]{1,0:T(1,128)S(1)} %copy-done.6), custom_call_target="tpu_custom_call" | custom-call | flops 409600 | bytes 409600 | tf_op jit(solution)/shard_map/faces/pallas_call | solution.py:188
  30.0 0.0 all-to-all-done.spec_ref
  30.0 0.0 copy-done.4
  30.1 0.7 %finish.1 = f32[5,4,1024]{2,1,0:T(4,128)} custom-call(f32[5,4,1024]{2,1,0:T(4,128)S(1)} %faces.1.part_ref, f32[4,5,4,1024]{3,2,1,0:T(4,128)S(1)} %all-to-all-done.spec_ref, f32[4,1024]{1,0:T(4,128)S(1)} %copy-done.4), custom_call_target="tpu_custom_call" | custom-call | flops 102400 | bytes 491520 | tf_op jit(solution)/shard_map/finish/pallas_call | solution.py:196
Async XLA Ops:
  0.0 11.9 %collective-permute-start.2 = (f32[5,4,1024]{2,1,0:T(4,128)}, f32[5,4,1024]{2,1,0:T(4,128)S(1)}, u32[]{:S(2)}, u32[]{:S(2)}) collective-permute-start(f32[5,4,1024]{2,1,0:T(4,128)} %bitcast.8), channel_id=1, source_target_pairs={{0,64},{64,0},{128,192},{192,128},{256,320},{320,256},{384,448},{4... | collective-permute-start | bytes 245768 | tf_op jit(solution)/shard_map/ppermute | solution.py:160
  4.4 1.4 %copy-start = (f32[1,4,5,5,4,1024]{5,4,3,2,1,0:T(4,128)S(1)}, f32[1,4,5,5,4,1024]{5,4,3,2,1,0:T(4,128)}, u32[]{:S(2)}) copy-start(f32[1,4,5,5,4,1024]{5,4,3,2,1,0:T(4,128)} %param.8) | copy-start | bytes 4915204
  5.9 0.9 %copy-start.3 = (f32[1,5,4,1024]{3,2,1,0:T(4,128)S(1)}, f32[1,5,4,1024]{3,2,1,0:T(4,128)}, u32[]{:S(2)}) copy-start(f32[1,5,4,1024]{3,2,1,0:T(4,128)} %param.7) | copy-start | bytes 245764
  6.7 21.0 %copy-start.1 = (f32[1,3,5,5,4,1024]{5,4,3,2,1,0:T(4,128)S(1)}, f32[1,3,5,5,4,1024]{5,4,3,2,1,0:T(4,128)}, u32[]{:S(2)}) copy-start(f32[1,3,5,5,4,1024]{5,4,3,2,1,0:T(4,128)} %param.9) | copy-start | bytes 3686404
  6.8 21.0 %copy-start.2 = (f32[1,5,4,1024]{3,2,1,0:T(4,128)S(1)}, f32[1,5,4,1024]{3,2,1,0:T(4,128)}, u32[]{:S(2)}) copy-start(f32[1,5,4,1024]{3,2,1,0:T(4,128)} %param.10) | copy-start | bytes 245764
  8.1 21.6 %copy-start.5 = (s32[1,1024]{1,0:T(1,128)S(1)}, s32[1,1024]{1,0:T(1,128)}, u32[]{:S(2)}) copy-start(s32[1,1024]{1,0:T(1,128)} %low_ref.1) | copy-start | bytes 12292
  8.1 21.6 %copy-start.6 = (s32[1,1024]{1,0:T(1,128)S(1)}, s32[1,1024]{1,0:T(1,128)}, u32[]{:S(2)}) copy-start(s32[1,1024]{1,0:T(1,128)} %up_ref.1) | copy-start | bytes 12292
  8.1 21.9 %copy-start.4 = (f32[4,1024]{1,0:T(4,128)S(1)}, f32[4,1024]{1,0:T(4,128)}, u32[]{:S(2)}) copy-start(f32[4,1024]{1,0:T(4,128)} %vol_ref.1) | copy-start | bytes 49156
  12.7 17.3 %all-to-all-start = ((f32[4,5,4,1024]{3,2,1,0:T(4,128)}), f32[4,5,4,1024]{3,2,1,0:T(4,128)S(1)}, u32[]{:S(2)}, u32[]{:S(2)}) async-start(f32[4,5,4,1024]{3,2,1,0:T(4,128)} %combine.1), calls=%async_computation | async-start | bytes 655360 | tf_op jit(solution)/shard_map/all_to_all | solution.py:176
  16.9 12.0 %collective-permute-start = (f32[5,2,1024]{2,1,0:T(2,128)S(1)}, f32[5,2,1024]{2,1,0:T(2,128)S(1)}, u32[]{:S(2)}, u32[]{:S(2)}) collective-permute-start(f32[5,2,1024]{2,1,0:T(2,128)S(1)} %get-tuple-element.11), channel_id=1, source_target_pairs={{0,1},{1,0},{2,3},{3,2},{4,5},{5,4},{6,7},{7,6},{8,9},{9,8},{10,11... | collective-permute-start | bytes 122888 | tf_op jit(solution)/shard_map/ppermute | solution.py:177
  20.1 9.5 %collective-permute-start.1 = (f32[5,2,1024]{2,1,0:T(2,128)S(1)}, f32[5,2,1024]{2,1,0:T(2,128)S(1)}, u32[]{:S(2)}, u32[]{:S(2)}) collective-permute-start(f32[5,2,1024]{2,1,0:T(2,128)S(1)} %get-tuple-element.12), channel_id=1, source_target_pairs={{1,2},{2,1},{3,4},{4,3},{5,6},{6,5},{7,8},{8,7},{9,10},{10,9},{11,... | collective-permute-start | bytes 122888 | tf_op jit(solution)/shard_map/ppermute | solution.py:170

commit v3 on v2

--- a/solution.py
+++ b/solution.py
@@ -59,33 +59,22 @@
         far_ref[b] = jnp.where(even, below, above)
 
 
-def along_kernel(own_ref, inner_ref, jac_hbm, obj_hbm, part_ref, jac, obj, side, sems):
-    copies = [pltpu.make_async_copy(jac_hbm.at[k], jac.at[k], sems.at[k]) for k in range(3)]
-    last = pltpu.make_async_copy(obj_hbm, obj, sems.at[3])
-    for copy in copies[1:]:
-        copy.start()
-    copies[0].start()
-    last.start()
+def along_kernel(own_ref, inner_ref, jac_ref, obj_ref, part_ref, side):
     cells = own_ref.shape[2]
     side[...] = jnp.zeros_like(side)
+    for at in range(0, cells, 128):
+        here = slice(at, at + 128)
+        fields = [own_ref[a, :, here] for a in range(NF)]
+        for b in range(NF):
+            part_ref[b, :, here] = obj_ref[b, :, here] + inner_ref[b, :, here] + products(fields, jac_ref, 0, b, here)
+            for k in (1, 2):
+                side[k - 1, b, 0:4, here] = products(fields, jac_ref, k, b, here)
     lane = lax.broadcasted_iota(jnp.int32, (8, cells), 1)
-    for k in (1, 2, 0):
-        copies[k].wait()
-        for at in range(0, cells, 128):
-            here = slice(at, at + 128)
-            fields = [own_ref[a, :, here] for a in range(NF)]
-            for b in range(NF):
-                total = products(fields, jac, k, b, here)
-                if k == 0:
-                    part_ref[b, :, here] = total
-                else:
-                    side[k - 1, b, 0:4, here] = total
-    last.wait()
     for b in range(NF):
         plus = jnp.where(lane == 0, 0.0, pltpu.roll(side[0, b], 1, 1))
         minus = jnp.where(lane == cells - 1, 0.0, pltpu.roll(side[1, b], cells - 1, 1))
         side[0, b] = plus + minus
-        part_ref[b] = part_ref[b] + obj[b] + inner_ref[b] + side[0, b, 0:4, :]
+        part_ref[b] = part_ref[b] + side[0, b, 0:4, :]
 
 
 def combine_kernel(own_ref, other_ref, out_ref):
@@ -96,6 +85,11 @@
         ours = float(table[0, 2 * j])
         theirs = jnp.where(odd, float(table[0, (2 * j + 1) % NT]), float(table[1, 2 * j]))
         out_ref[(at // 2 + j) % PAIRS] = ours * own_ref[...] + theirs * other_ref[...]
+
+
+def after_kernel(near_ref, far_ref, near_out_ref, far_out_ref):
+    near_out_ref[...] = near_ref[...]
+    far_out_ref[...] = far_ref[...]
 
 
 def faces_kernel(part_ref, near_ref, far_ref, low_ref, up_ref, out_ref, halo, moved):
@@ -166,24 +160,18 @@
             pltpu.SemaphoreType.DMA((5,)),
         ],
         limit=3 * 2**20, flops=40 * block, moved=84 * block,
-    )(adjoint[0], jac_x[0])
+    )(pltpu.with_memory_space_constraint(adjoint[0], pltpu.HBM), pltpu.with_memory_space_constraint(jac_x[0], pltpu.HBM))
     far = lax.ppermute(far, "space", [pair for i in range(1, count - 1, 2) for pair in ((i, i + 1), (i + 1, i))])
     combined = kernel_call(
-        combine_kernel, "combine", jax.ShapeDtypeStruct((PAIRS, NF, layers, cells), jnp.float32), [VMEM, VMEM],
-        flops=12 * block, moved=24 * block,
+        combine_kernel, "combine", jax.ShapeDtypeStruct((PAIRS, NF, layers, cells), jnp.float32), [VMEM] * 2,
+        moved=2000 * block,
     )(own, other)
     groups = [list(range(parity, NT, 2)) for parity in range(2)]
     spectral = lax.all_to_all(combined, "tm", 0, 0, tiled=True, axis_index_groups=groups)
+    near, far = kernel_call(after_kernel, "after", (face, face), [VMEM] * 2, flops=10**11, moved=10**8)(near, far)
     near = lax.ppermute(near, "space", [(i, i ^ 1) for i in range(count)])
     part = kernel_call(
-        along_kernel, "along", field, [VMEM, VMEM, HBM, HBM],
-        [
-            pltpu.VMEM((3, NF, NF, layers, cells), jnp.float32),
-            pltpu.VMEM((NF, layers, cells), jnp.float32),
-            pltpu.VMEM((2, NF, 8, cells), jnp.float32),
-            pltpu.SemaphoreType.DMA((4,)),
-        ],
-        limit=3 * 2**20, flops=30 * block, moved=80 * block,
+        along_kernel, "along", field, [VMEM] * 4, [pltpu.VMEM((2, NF, 8, cells), jnp.float32)],
     )(own, inner, jac_local[0], objective_gradient[0])
     part = kernel_call(
         faces_kernel, "faces", field, [VMEM] * 5,

time: 31 us -> 27 us (0.87)
  the two profiles are of different devices: /device:TPU:251 before, /device:TPU:2 now
where the time goes in v3:
time: 27 us; the launch traced here: 26.8 us
  starting transfers between devices  18.5 us (69%)
  waiting for transfers between devices  4.47 us (17%)
  Pallas kernels  3.67 us (14%)
    all_to_all x1, starting transfers between devices, body(): lax.all_to_all(combined, 'tm', 0, 0, tiled=True, axis_index_groups=groups)  8.1 us
    ppermute x1, starting transfers between devices, body(): other = lax.ppermute(adjoint[0], 'tm', [(i, i ^ 1) for i in range(NT)])  7.72 us
    ppermute x1, starting transfers between devices, body(): near = lax.ppermute(near, 'space', [(i, i ^ 1) for i in range(count)])  2.05 us
    all_to_all x1, waiting for transfers between devices, body(): lax.all_to_all(combined, 'tm', 0, 0, tiled=True, axis_index_groups=groups)  1.91 us
    ppermute x1, waiting for transfers between devices, body(): other = lax.ppermute(adjoint[0], 'tm', [(i, i ^ 1) for i in range(NT)])  1.68 us
    pallas_call x1, Pallas kernels, body(): kernel_call(across_kernel, 'across', (field, field, face, face), [HBM, HB...  1.59 us
    ppermute x1, waiting for transfers between devices, body(): near = lax.ppermute(near, 'space', [(i, i ^ 1) for i in range(count)])  0.87 us
    pallas_call x1, Pallas kernels, body(): kernel_call(combine_kernel, 'combine', jax.ShapeDtypeStruct((PAIRS, NF, l...  0.78 us
  transfers between devices with their start and end apart: 4, of which 3 were waited for; matrix products, arithmetic and copies ran while one was open for 0% of the time, Pallas kernels for 11%

profile of v3, /device:TPU:2, one launch (start us, length us, event | category | flops | bytes accessed | tf_op | source)
XLA Modules:
  0.0 26.8 jit_solution(3476839366803278384)
XLA Ops:
  0.0 7.7 %collective-permute-start.2 = (f32[5,4,1024]{2,1,0:T(4,128)}, f32[5,4,1024]{2,1,0:T(4,128)S(1)}, u32[]{:S(2)}, u32[]{:S(2)}) collective-permute-start(f32[5,4,1024]{2,1,0:T(4,128)} %bitcast.8), channel_id=1, source_target_pairs={{0,64},{64,0},{128,192},{192,128},{256,320},{320,256},{384,448},{4... | collective-permute-start | bytes 245768 | tf_op jit(solution)/shard_map/ppermute | solution.py:154
  7.7 1.6 %across.1 = (f32[5,4,1024]{2,1,0:T(4,128)S(1)}, f32[5,4,1024]{2,1,0:T(4,128)S(1)}, f32[5,2,1024]{2,1,0:T(2,128)S(1)}, f32[5,2,1024]{2,1,0:T(2,128)S(1)}) custom-call(f32[5,4,1024]{2,1,0:T(4,128)} %bitcast.9, f32[4,5,5,4,1024]{4,3,2,1,0:T(4,128)} %bitcast.7), custom_call_target="tpu_custom_call" | custom-call | flops 819200 | bytes 1720320 | tf_op jit(solution)/shard_map/across/pallas_call | solution.py:155
  9.3 0.7 %collective-permute-start = (f32[5,2,1024]{2,1,0:T(2,128)S(1)}, f32[5,2,1024]{2,1,0:T(2,128)S(1)}, u32[]{:S(2)}, u32[]{:S(2)}) collective-permute-start(f32[5,2,1024]{2,1,0:T(2,128)S(1)} %get-tuple-element.14), channel_id=1, source_target_pairs={{1,2},{2,1},{3,4},{4,3},{5,6},{6,5},{7,8},{8,7},{9,10},{10,9},{11,... | collective-permute-start | bytes 122888 | tf_op jit(solution)/shard_map/ppermute | solution.py:164
  10.0 1.7 %collective-permute-done.2.other_ref = f32[5,4,1024]{2,1,0:T(4,128)S(1)} collective-permute-done((f32[5,4,1024]{2,1,0:T(4,128)}, f32[5,4,1024]{2,1,0:T(4,128)S(1)}, u32[]{:S(2)}, u32[]{:S(2)}) %collective-permute-start.2) | collective-permute-done | bytes 81952 | tf_op jit(solution)/shard_map/ppermute | solution.py:154
  11.7 0.8 %combine.1 = f32[4,5,4,1024]{3,2,1,0:T(4,128)} custom-call(f32[5,4,1024]{2,1,0:T(4,128)S(1)} %get-tuple-element.11.own_ref, f32[5,4,1024]{2,1,0:T(4,128)S(1)} %collective-permute-done.2.other_ref), custom_call_target="tpu_custom_call" | custom-call | bytes 40960000 | tf_op jit(solution)/shard_map/combine/pallas_call | solution.py:165
  12.5 8.1 %all-to-all-start = ((f32[4,5,4,1024]{3,2,1,0:T(4,128)}), f32[4,5,4,1024]{3,2,1,0:T(4,128)S(1)}, u32[]{:S(2)}, u32[]{:S(2)}) async-start(f32[4,5,4,1024]{3,2,1,0:T(4,128)} %combine.1), calls=%async_computation | async-start | bytes 655360 | tf_op jit(solution)/shard_map/all_to_all | solution.py:170
  20.6 0.0 collective-permute-done.far_ref
  20.6 0.0 copy-start
  20.6 0.0 copy-start.1
  20.6 0.0 copy-start.3
  20.6 0.0 copy-start.4
  20.6 0.0 copy-start.2
  20.6 2.1 %collective-permute-start.1 = (f32[5,2,1024]{2,1,0:T(2,128)S(1)}, f32[5,2,1024]{2,1,0:T(2,128)S(1)}, u32[]{:S(2)}, u32[]{:S(2)}) collective-permute-start(f32[5,2,1024]{2,1,0:T(2,128)S(1)} %get-tuple-element.15), channel_id=1, source_target_pairs={{0,1},{1,0},{2,3},{3,2},{4,5},{5,4},{6,7},{7,6},{8,9},{9,8},{10,11... | collective-permute-start | bytes 122888 | tf_op jit(solution)/shard_map/ppermute | solution.py:172
  22.7 0.0 copy-done
  22.7 0.0 copy-done.1
  22.7 0.3 %along.1.part_ref = f32[5,4,1024]{2,1,0:T(4,128)S(1)} custom-call(f32[5,4,1024]{2,1,0:T(4,128)S(1)} %get-tuple-element.11.own_ref, f32[5,4,1024]{2,1,0:T(4,128)S(1)} %get-tuple-element.12.inner_ref, f32[3,5,5,4,1024]{4,3,2,1,0:T(4,128)S(1)} %bitcast.5, f32[5,4,1024]{2,1,0:T(4,128)S(1)} %bitcast.6), custom_call_target="tpu_custom_call" | custom-call | tf_op jit(solution)/shard_map/along/pallas_call | solution.py:173
  23.0 0.9 %collective-permute-done.1.near_ref = f32[5,2,1024]{2,1,0:T(2,128)S(1)} collective-permute-done((f32[5,2,1024]{2,1,0:T(2,128)S(1)}, f32[5,2,1024]{2,1,0:T(2,128)S(1)}, u32[]{:S(2)}, u32[]{:S(2)}) %collective-permute-start.1) | collective-permute-done | bytes 40992 | tf_op jit(solution)/shard_map/ppermute | solution.py:172
  23.9 0.0 copy-done.3
  23.9 0.0 copy-done.4
  23.9 0.3 %faces.1.part_ref = f32[5,4,1024]{2,1,0:T(4,128)S(1)} custom-call(f32[5,4,1024]{2,1,0:T(4,128)S(1)} %along.1.part_ref, f32[5,2,1024]{2,1,0:T(2,128)S(1)} %collective-permute-done.1.near_ref, f32[5,2,1024]{2,1,0:T(2,128)S(1)} %get-tuple-element.16.far_ref, s32[1,1024]{1,0:T(1,128)S(1)} %copy-done.3, s32[1,1024]{1,0:T(1,128)S(1)} %copy-done.4), custom_call_target="tpu_custom_call" | custom-call | flops 409600 | bytes 409600 | tf_op jit(solution)/shard_map/faces/pallas_call | solution.py:176
  24.2 1.9 %all-to-all-done.spec_ref = f32[4,5,4,1024]{3,2,1,0:T(4,128)S(1)} async-done(((f32[4,5,4,1024]{3,2,1,0:T(4,128)}), f32[4,5,4,1024]{3,2,1,0:T(4,128)S(1)}, u32[]{:S(2)}, u32[]{:S(2)}) %all-to-all-start) | async-done | bytes 327712 | tf_op jit(solution)/shard_map/all_to_all | solution.py:170
  26.1 0.0 copy-done.2
  26.1 0.7 %finish.1 = f32[5,4,1024]{2,1,0:T(4,128)} custom-call(f32[5,4,1024]{2,1,0:T(4,128)S(1)} %faces.1.part_ref, f32[4,5,4,1024]{3,2,1,0:T(4,128)S(1)} %all-to-all-done.spec_ref, f32[4,1024]{1,0:T(4,128)S(1)} %copy-done.2), custom_call_target="tpu_custom_call" | custom-call | flops 102400 | bytes 491520 | tf_op jit(solution)/shard_map/finish/pallas_call | solution.py:184
  (1 shorter events, 0.0 us)
Async XLA Ops:
  0.0 11.7 %collective-permute-start.2 = (f32[5,4,1024]{2,1,0:T(4,128)}, f32[5,4,1024]{2,1,0:T(4,128)S(1)}, u32[]{:S(2)}, u32[]{:S(2)}) collective-permute-start(f32[5,4,1024]{2,1,0:T(4,128)} %bitcast.8), channel_id=1, source_target_pairs={{0,64},{64,0},{128,192},{192,128},{256,320},{320,256},{384,448},{4... | collective-permute-start | bytes 245768 | tf_op jit(solution)/shard_map/ppermute | solution.py:154
  9.3 11.2 %collective-permute-start = (f32[5,2,1024]{2,1,0:T(2,128)S(1)}, f32[5,2,1024]{2,1,0:T(2,128)S(1)}, u32[]{:S(2)}, u32[]{:S(2)}) collective-permute-start(f32[5,2,1024]{2,1,0:T(2,128)S(1)} %get-tuple-element.14), channel_id=1, source_target_pairs={{1,2},{2,1},{3,4},{4,3},{5,6},{6,5},{7,8},{8,7},{9,10},{10,9},{11,... | collective-permute-start | bytes 122888 | tf_op jit(solution)/shard_map/ppermute | solution.py:164
  12.5 13.7 %all-to-all-start = ((f32[4,5,4,1024]{3,2,1,0:T(4,128)}), f32[4,5,4,1024]{3,2,1,0:T(4,128)S(1)}, u32[]{:S(2)}, u32[]{:S(2)}) async-start(f32[4,5,4,1024]{3,2,1,0:T(4,128)} %combine.1), calls=%async_computation | async-start | bytes 655360 | tf_op jit(solution)/shard_map/all_to_all | solution.py:170
  20.6 2.1 %copy-start = (f32[1,3,5,5,4,1024]{5,4,3,2,1,0:T(4,128)S(1)}, f32[1,3,5,5,4,1024]{5,4,3,2,1,0:T(4,128)}, u32[]{:S(2)}) copy-start(f32[1,3,5,5,4,1024]{5,4,3,2,1,0:T(4,128)} %param.9) | copy-start | bytes 3686404
  20.6 2.1 %copy-start.1 = (f32[1,5,4,1024]{3,2,1,0:T(4,128)S(1)}, f32[1,5,4,1024]{3,2,1,0:T(4,128)}, u32[]{:S(2)}) copy-start(f32[1,5,4,1024]{3,2,1,0:T(4,128)} %param.10) | copy-start | bytes 245764
  20.6 3.3 %copy-start.3 = (s32[1,1024]{1,0:T(1,128)S(1)}, s32[1,1024]{1,0:T(1,128)}, u32[]{:S(2)}) copy-start(s32[1,1024]{1,0:T(1,128)} %low_ref.1) | copy-start | bytes 12292
  20.6 3.3 %copy-start.4 = (s32[1,1024]{1,0:T(1,128)S(1)}, s32[1,1024]{1,0:T(1,128)}, u32[]{:S(2)}) copy-start(s32[1,1024]{1,0:T(1,128)} %up_ref.1) | copy-start | bytes 12292
  20.6 5.5 %copy-start.2 = (f32[4,1024]{1,0:T(4,128)S(1)}, f32[4,1024]{1,0:T(4,128)}, u32[]{:S(2)}) copy-start(f32[4,1024]{1,0:T(4,128)} %vol_ref.1) | copy-start | bytes 49156
  20.6 3.2 %collective-permute-start.1 = (f32[5,2,1024]{2,1,0:T(2,128)S(1)}, f32[5,2,1024]{2,1,0:T(2,128)S(1)}, u32[]{:S(2)}, u32[]{:S(2)}) collective-permute-start(f32[5,2,1024]{2,1,0:T(2,128)S(1)} %get-tuple-element.15), channel_id=1, source_target_pairs={{0,1},{1,0},{2,3},{3,2},{4,5},{5,4},{6,7},{7,6},{8,9},{9,8},{10,11... | collective-permute-start | bytes 122888 | tf_op jit(solution)/shard_map/ppermute | solution.py:172

commit v4 on v3

--- a/solution.py
+++ b/solution.py
@@ -10,7 +10,6 @@
 NF = 5
 PAIRS = NT // 2
 VMEM = pl.BlockSpec(memory_space=pltpu.VMEM)
-HBM = pl.BlockSpec(memory_space=pltpu.HBM)
 
 
 def spectral_table(count):
@@ -34,21 +33,18 @@
     return total
 
 
-def across_kernel(adj_hbm, jac_hbm, own_ref, inner_ref, near_ref, far_ref, jac, ext, sems):
-    first = pltpu.make_async_copy(adj_hbm, own_ref, sems.at[0])
-    first.start()
-    copies = [pltpu.make_async_copy(jac_hbm.at[k], jac.at[k], sems.at[1 + k]) for k in range(4)]
-    for copy in copies:
-        copy.start()
+def zeros_kernel(out_ref):
+    out_ref[...] = jnp.zeros_like(out_ref)
+
+
+def across_kernel(zeros_ref, own_ref, jac, inner_ref, near_ref, far_ref, ext):
     cells = own_ref.shape[2]
-    ext[...] = jnp.zeros_like(ext)
-    first.wait()
-    for k, offset in enumerate((1, -1, 2, -2)):
-        copies[k].wait()
-        for at in range(0, cells, 128):
-            here = slice(at, at + 128)
-            fields = [own_ref[a, :, here] for a in range(NF)]
-            for b in range(NF):
+    for at in range(0, cells, 128):
+        here = slice(at, at + 128)
+        fields = [own_ref[a, :, here] for a in range(NF)]
+        for b in range(NF):
+            ext[b, :, here] = zeros_ref[...]
+            for k, offset in enumerate((1, -1, 2, -2)):
                 ext[b, 2 + offset:6 + offset, here] += products(fields, jac, k, b, here)
     even = lax.axis_index("space") % 2 == 0
     for b in range(NF):
@@ -92,14 +88,16 @@
     far_out_ref[...] = far_ref[...]
 
 
-def faces_kernel(part_ref, near_ref, far_ref, low_ref, up_ref, out_ref, halo, moved):
+def faces_kernel(part_ref, spec_ref, vol_ref, near_ref, far_ref, low_ref, up_ref, out_ref, halo, moved):
     odd = lax.axis_index("space") % 2 == 1
     cells = low_ref.shape[1]
     halo[...] = jnp.zeros_like(halo)
+    sibling = 1 - lax.axis_index("space") % 2
     for b in range(NF):
         row = 4 * (b % 2)
-        halo[b // 2, row:row + 2, :] = jnp.where(odd, near_ref[b], far_ref[b])
-        halo[b // 2, row + 2:row + 4, :] = jnp.where(odd, far_ref[b], near_ref[b])
+        near = near_ref[sibling, b]
+        halo[b // 2, row:row + 2, :] = jnp.where(odd, near, far_ref[b])
+        halo[b // 2, row + 2:row + 4, :] = jnp.where(odd, far_ref[b], near)
     groups = halo.shape[0]
     chunks = cells // 128
     from_low = lax.broadcasted_iota(jnp.int32, (8, 128), 0) % 4 < 2
@@ -116,9 +114,13 @@
                 piece = jnp.take_along_axis(halo[g, :, 128 * c:128 * (c + 1)], lane, axis=1, mode="promise_in_bounds")
                 total = piece if c == 0 else jnp.where(chunk == c, piece, total)
             moved[g, :, here] = total
+    scale = 1.5 * vol_ref[...]
     for b in range(NF):
         row = 4 * (b % 2)
-        out_ref[b] = part_ref[b] + moved[b // 2, row:row + 4, :]
+        spectral = spec_ref[0, b]
+        for j in range(1, PAIRS):
+            spectral = spectral + spec_ref[j, b]
+        out_ref[b] = part_ref[b] + moved[b // 2, row:row + 4, :] + scale * spectral
 
 
 def finish_kernel(part_ref, spec_ref, vol_ref, out_ref):
@@ -152,38 +154,49 @@
     field = jax.ShapeDtypeStruct((NF, layers, cells), jnp.float32)
     face = jax.ShapeDtypeStruct((NF, 2, cells), jnp.float32)
     other = lax.ppermute(adjoint[0], "tm", [(i, i ^ 1) for i in range(NT)])
-    own, inner, near, far = kernel_call(
-        across_kernel, "across", (field, field, face, face), [HBM, HBM],
-        [
-            pltpu.VMEM((4, NF, NF, layers, cells), jnp.float32),
-            pltpu.VMEM((NF, 8, cells), jnp.float32),
-            pltpu.SemaphoreType.DMA((5,)),
-        ],
-        limit=3 * 2**20, flops=40 * block, moved=84 * block,
-    )(pltpu.with_memory_space_constraint(adjoint[0], pltpu.HBM), pltpu.with_memory_space_constraint(jac_x[0], pltpu.HBM))
+    zeros = kernel_call(zeros_kernel, "zeros", jax.ShapeDtypeStruct((8, 128), jnp.float32), [], flops=10**11)()
+    own = adjoint[0]
+    inner, near, far = kernel_call(
+        across_kernel, "across", (field, face, face), [VMEM] * 3, [pltpu.VMEM((NF, 8, cells), jnp.float32)],
+        flops=40 * block, moved=84 * block,
+    )(zeros, own, jac_x[0])
     far = lax.ppermute(far, "space", [pair for i in range(1, count - 1, 2) for pair in ((i, i + 1), (i + 1, i))])
-    combined = kernel_call(
-        combine_kernel, "combine", jax.ShapeDtypeStruct((PAIRS, NF, layers, cells), jnp.float32), [VMEM] * 2,
-        moved=2000 * block,
-    )(own, other)
     groups = [list(range(parity, NT, 2)) for parity in range(2)]
-    spectral = lax.all_to_all(combined, "tm", 0, 0, tiled=True, axis_index_groups=groups)
-    near, far = kernel_call(after_kernel, "after", (face, face), [VMEM] * 2, flops=10**11, moved=10**8)(near, far)
-    near = lax.ppermute(near, "space", [(i, i ^ 1) for i in range(count)])
+    pairs = [[i, i + 1] for i in range(0, count, 2)]
+    late = lax.axis_index("space") < 2
+
+    def swap(near):
+        return lax.all_gather(near, "space", axis=0, axis_index_groups=pairs)
+
+    def exchange(own, other):
+        combined = kernel_call(
+            combine_kernel, "combine", jax.ShapeDtypeStruct((PAIRS, NF, layers, cells), jnp.float32), [VMEM] * 2,
+            flops=12 * block, moved=24 * block,
+        )(own, other)
+        return lax.all_to_all(combined, "tm", 0, 0, tiled=True, axis_index_groups=groups)
+
+    def no_swap(near):
+        return jnp.zeros((2, *near.shape), near.dtype)
+
+    def in_turn(own, other, near, swapped):
+        return exchange(own, other), swapped
+
+    def together(own, other, near, swapped):
+        return exchange(own, other), swap(near)
+
     part = kernel_call(
         along_kernel, "along", field, [VMEM] * 4, [pltpu.VMEM((2, NF, 8, cells), jnp.float32)],
     )(own, inner, jac_local[0], objective_gradient[0])
-    part = kernel_call(
-        faces_kernel, "faces", field, [VMEM] * 5,
+    swapped = lax.cond(late, swap, no_swap, near)
+    spectral, near = lax.cond(late, in_turn, together, own, other, near, swapped)
+    out = kernel_call(
+        faces_kernel, "faces", field, [VMEM] * 7,
         [
             pltpu.VMEM(((NF + 1) // 2, 8, cells), jnp.float32),
             pltpu.VMEM(((NF + 1) // 2, 8, cells), jnp.float32),
         ],
         flops=20 * block, moved=20 * block,
-    )(part, near, far, face_lower, face_upper)
-    out = kernel_call(
-        finish_kernel, "finish", field, [VMEM] * 3, flops=5 * block, moved=24 * block,
-    )(part, spectral, volume)
+    )(part, spectral, volume, near, far, face_lower, face_upper)
     return out[None]
 
 

time: 27 us -> 26.2 us (0.970)
  the two profiles are of different devices: /device:TPU:2 before, /device:TPU:217 now
where the time goes in v4:
time: 26.2 us; the launch traced here: 26 us
  starting transfers between devices  17.3 us (66%)
  waiting for transfers between devices  4.03 us (15%)
  Pallas kernels  2.59 us (10%)
  blocking collectives  1.85 us (7%)
    ppermute x1, starting transfers between devices, body(): lax.ppermute(far, 'space', [pair for i in range(1, count - 1, 2) for pair...  8.41 us
    ppermute x1, starting transfers between devices, body(): other = lax.ppermute(adjoint[0], 'tm', [(i, i ^ 1) for i in range(NT)])  4.88 us
    all_to_all x1, waiting for transfers between devices, exchange(): lax.all_to_all(combined, 'tm', 0, 0, tiled=True, axis_index_groups=groups)  4.03 us
    all_to_all x1, starting transfers between devices, exchange(): lax.all_to_all(combined, 'tm', 0, 0, tiled=True, axis_index_groups=groups)  4.01 us
    all_gather x1, blocking collectives, swap(): return lax.all_gather(near, 'space', axis=0, axis_index_groups=pairs)  1.85 us
    pallas_call x1, Pallas kernels, body(): kernel_call(faces_kernel, 'faces', field, [VMEM] * 7, [pltpu.VMEM(((NF +...  1 us
    pallas_call x1, Pallas kernels, exchange(): kernel_call(combine_kernel, 'combine', jax.ShapeDtypeStruct((PAIRS, NF, l...  0.78 us
  transfers between devices with their start and end apart: 3, of which 1 were waited for; matrix products, arithmetic and copies ran while one was open for 0% of the time, Pallas kernels for 6%

profile of v4, /device:TPU:217, one launch (start us, length us, event | category | flops | bytes accessed | tf_op | source)
XLA Modules:
  0.0 26.0 jit_solution(1921589522133997873)
XLA Ops:
  0.0 0.0 copy-start
  0.0 0.0 copy-start.6
  0.0 4.9 %collective-permute-start = (f32[5,4,1024]{2,1,0:T(4,128)}, f32[5,4,1024]{2,1,0:T(4,128)S(1)}, u32[]{:S(2)}, u32[]{:S(2)}) collective-permute-start(f32[5,4,1024]{2,1,0:T(4,128)} %bitcast.10), channel_id=1, source_target_pairs={{0,64},{64,0},{128,192},{192,128},{256,320},{320,256},{384,448},{4... | collective-permute-start | bytes 245768 | tf_op jit(solution)/shard_map/ppermute | solution.py:156
  4.9 0.0 copy-start.1
  4.9 0.0 copy-start.2
  4.9 0.0 copy-done
  4.9 0.0 copy-done.6
  4.9 0.5 %across.1 = (f32[5,4,1024]{2,1,0:T(4,128)S(1)}, f32[5,2,1024]{2,1,0:T(2,128)S(1)}, f32[5,2,1024]{2,1,0:T(2,128)S(1)}) custom-call(f32[8,128]{1,0:T(8,128)S(1)} %zeros.1.zeros_ref, f32[5,4,1024]{2,1,0:T(4,128)S(1)} %bitcast.11, f32[4,5,5,4,1024]{4,3,2,1,0:T(4,128)S(1)} %bitcast.7), custom_call_target="tpu_custom_call" | custom-call | flops 819200 | bytes 1720320 | tf_op jit(solution)/shard_map/across/pallas_call | solution.py:159
  5.5 8.4 %collective-permute-start.1 = (f32[5,2,1024]{2,1,0:T(2,128)S(1)}, f32[5,2,1024]{2,1,0:T(2,128)S(1)}, u32[]{:S(2)}, u32[]{:S(2)}) collective-permute-start(f32[5,2,1024]{2,1,0:T(2,128)S(1)} %get-tuple-element.36), channel_id=1, source_target_pairs={{1,2},{2,1},{3,4},{4,3},{5,6},{6,5},{7,8},{8,7},{9,10},{10,9},{11,... | collective-permute-start | bytes 122888 | tf_op jit(solution)/shard_map/ppermute | solution.py:163
  13.9 0.0 copy-done.1
  13.9 0.0 copy-done.2
  13.9 0.3 %along.1.part_ref = f32[5,4,1024]{2,1,0:T(4,128)S(1)} custom-call(f32[5,4,1024]{2,1,0:T(4,128)S(1)} %bitcast.12, f32[5,4,1024]{2,1,0:T(4,128)S(1)} %get-tuple-element.32.inner_ref, f32[3,5,5,4,1024]{4,3,2,1,0:T(4,128)S(1)} %bitcast.8, f32[5,4,1024]{2,1,0:T(4,128)S(1)} %bitcast.9), custom_call_target="tpu_custom_call" | custom-call | tf_op jit(solution)/shard_map/along/pallas_call | solution.py:187
  14.2 0.0 copy-start.3
  14.2 0.0 copy-start.4
  14.2 0.0 copy-start.5
  14.3 0.0 collective-permute-done
  14.3 10.7 %conditional.3 = (f32[4,5,4,1024]{3,2,1,0:T(4,128)S(1)}, f32[2,5,2,1024]{3,2,1,0:T(2,128)S(1)}) conditional(s32[]{:T(128)} %convert_element_type.4, (f32[5,4,1024]{2,1,0:T(4,128)S(1)}, f32[5,4,1024]{2,1,0:T(4,128)S(1)}, f32[5,2,1024]{2,1,0:T(2,128)S(1)}) %tuple.26, (f32[5,4,1024]{2,1,0:T(4,128)S(1)}, f32[5,4,1024]{2,1,0:T(4,128)S(1)}, ...), branch_computations={%region_2.0_spmd, %region_3.0_spmd} | conditional | flops 245760 | bytes 1597488 | solution.py:191
  14.3 0.8 %combine.2 = f32[4,5,4,1024]{3,2,1,0:T(4,128)} custom-call(f32[5,4,1024]{2,1,0:T(4,128)S(1)} %get-tuple-element.21.own_ref, f32[5,4,1024]{2,1,0:T(4,128)S(1)} %get-tuple-element.22.other_ref), custom_call_target="tpu_custom_call" | custom-call | flops 245760 | bytes 491520 | tf_op jit(solution)/shard_map/cond/branch_0_fun/combine/pallas_call | solution.py:172
  15.1 4.0 %all-to-all-start = ((f32[4,5,4,1024]{3,2,1,0:T(4,128)}), f32[4,5,4,1024]{3,2,1,0:T(4,128)S(1)}, u32[]{:S(2)}, u32[]{:S(2)}) async-start(f32[4,5,4,1024]{3,2,1,0:T(4,128)} %combine.2), calls=%async_computation | async-start | bytes 655360 | tf_op jit(solution)/shard_map/cond/branch_0_fun/all_to_all | solution.py:176
  19.1 1.9 %all-gather.1 = f32[10,2,1024]{2,1,0:T(2,128)S(1)} all-gather(f32[5,2,1024]{2,1,0:T(2,128)S(1)} %get-tuple-element.23), channel_id=3, replica_groups={{0,1},{2,3},{4,5},{6,7},{8,9},{10,11},{12,13},{14,15},{16,17},{18,19},{..., dimensions={0}, use_global_device_ids=true | all-gather | bytes 122880 | tf_op jit(solution)/shard_map/cond/branch_0_fun/all_gather | solution.py:169
  21.0 4.0 %all-to-all-done = f32[4,5,4,1024]{3,2,1,0:T(4,128)S(1)} async-done(((f32[4,5,4,1024]{3,2,1,0:T(4,128)}), f32[4,5,4,1024]{3,2,1,0:T(4,128)S(1)}, u32[]{:S(2)}, u32[]{:S(2)}) %all-to-all-start) | async-done | bytes 327712 | tf_op jit(solution)/shard_map/cond/branch_0_fun/all_to_all | solution.py:176
  25.0 0.0 collective-permute-done.1.far_ref
  25.0 0.0 copy-done.3
  25.0 0.0 copy-done.4
  25.0 0.0 copy-done.5
  25.0 1.0 %faces.1 = f32[5,4,1024]{2,1,0:T(4,128)} custom-call(f32[5,4,1024]{2,1,0:T(4,128)S(1)} %along.1.part_ref, f32[4,5,4,1024]{3,2,1,0:T(4,128)S(1)} %get-tuple-element.34.spec_ref, f32[4,1024]{1,0:T(4,128)S(1)} %copy-done.3, f32[2,5,2,1024]{3,2,1,0:T(2,128)S(1)} %get-tuple-element.35.near_ref, f32[5,2,1024]{2,1,0:T(2,128)S(1)} %collective-permute-done.1.far_ref, ...), custom_call_target="tpu_custom_call" | custom-call | flops 409600 | bytes 409600 | tf_op jit(solution)/shard_map/faces/pallas_call | solution.py:192
  (3 shorter events, 0.1 us)
Async XLA Ops:
  0.0 4.9 %copy-start = (f32[1,4,5,5,4,1024]{5,4,3,2,1,0:T(4,128)S(1)}, f32[1,4,5,5,4,1024]{5,4,3,2,1,0:T(4,128)}, u32[]{:S(2)}) copy-start(f32[1,4,5,5,4,1024]{5,4,3,2,1,0:T(4,128)} %param.12) | copy-start | bytes 4915204
  0.0 4.9 %copy-start.6 = (f32[1,5,4,1024]{3,2,1,0:T(4,128)S(1)}, f32[1,5,4,1024]{3,2,1,0:T(4,128)}, u32[]{:S(2)}) copy-start(f32[1,5,4,1024]{3,2,1,0:T(4,128)} %param.11) | copy-start | bytes 245764
  0.0 14.3 %collective-permute-start = (f32[5,4,1024]{2,1,0:T(4,128)}, f32[5,4,1024]{2,1,0:T(4,128)S(1)}, u32[]{:S(2)}, u32[]{:S(2)}) collective-permute-start(f32[5,4,1024]{2,1,0:T(4,128)} %bitcast.10), channel_id=1, source_target_pairs={{0,64},{64,0},{128,192},{192,128},{256,320},{320,256},{384,448},{4... | collective-permute-start | bytes 245768 | tf_op jit(solution)/shard_map/ppermute | solution.py:156
  4.9 9.0 %copy-start.1 = (f32[1,3,5,5,4,1024]{5,4,3,2,1,0:T(4,128)S(1)}, f32[1,3,5,5,4,1024]{5,4,3,2,1,0:T(4,128)}, u32[]{:S(2)}) copy-start(f32[1,3,5,5,4,1024]{5,4,3,2,1,0:T(4,128)} %param.13) | copy-start | bytes 3686404
  4.9 9.0 %copy-start.2 = (f32[1,5,4,1024]{3,2,1,0:T(4,128)S(1)}, f32[1,5,4,1024]{3,2,1,0:T(4,128)}, u32[]{:S(2)}) copy-start(f32[1,5,4,1024]{3,2,1,0:T(4,128)} %param.14) | copy-start | bytes 245764
  5.5 19.5 %collective-permute-start.1 = (f32[5,2,1024]{2,1,0:T(2,128)S(1)}, f32[5,2,1024]{2,1,0:T(2,128)S(1)}, u32[]{:S(2)}, u32[]{:S(2)}) collective-permute-start(f32[5,2,1024]{2,1,0:T(2,128)S(1)} %get-tuple-element.36), channel_id=1, source_target_pairs={{1,2},{2,1},{3,4},{4,3},{5,6},{6,5},{7,8},{8,7},{9,10},{10,9},{11,... | collective-permute-start | bytes 122888 | tf_op jit(solution)/shard_map/ppermute | solution.py:163
  14.2 10.8 %copy-start.3 = (f32[4,1024]{1,0:T(4,128)S(1)}, f32[4,1024]{1,0:T(4,128)}, u32[]{:S(2)}) copy-start(f32[4,1024]{1,0:T(4,128)} %vol_ref.1) | copy-start | bytes 49156
  14.2 10.8 %copy-start.4 = (s32[1,1024]{1,0:T(1,128)S(1)}, s32[1,1024]{1,0:T(1,128)}, u32[]{:S(2)}) copy-start(s32[1,1024]{1,0:T(1,128)} %low_ref.1) | copy-start | bytes 12292
  14.2 10.8 %copy-start.5 = (s32[1,1024]{1,0:T(1,128)S(1)}, s32[1,1024]{1,0:T(1,128)}, u32[]{:S(2)}) copy-start(s32[1,1024]{1,0:T(1,128)} %up_ref.1) | copy-start | bytes 12292
  15.1 9.9 %all-to-all-start = ((f32[4,5,4,1024]{3,2,1,0:T(4,128)}), f32[4,5,4,1024]{3,2,1,0:T(4,128)S(1)}, u32[]{:S(2)}, u32[]{:S(2)}) async-start(f32[4,5,4,1024]{3,2,1,0:T(4,128)} %combine.2), calls=%async_computation | async-start | bytes 655360 | tf_op jit(solution)/shard_map/cond/branch_0_fun/all_to_all | solution.py:176

commit v5 on v4

--- a/solution.py
+++ b/solution.py
@@ -163,10 +163,17 @@
     far = lax.ppermute(far, "space", [pair for i in range(1, count - 1, 2) for pair in ((i, i + 1), (i + 1, i))])
     groups = [list(range(parity, NT, 2)) for parity in range(2)]
     pairs = [[i, i + 1] for i in range(0, count, 2)]
-    late = lax.axis_index("space") < 2
+    space = lax.axis_index("space")
+    edge = jnp.logical_and(space >= 2, jnp.logical_or(space % 8 < 2, space % 8 >= 6))
+    late = jnp.logical_not(edge)
 
     def swap(near):
         return lax.all_gather(near, "space", axis=0, axis_index_groups=pairs)
+
+    def along(own, inner, jac, gradient):
+        return kernel_call(
+            along_kernel, "along", field, [VMEM] * 4, [pltpu.VMEM((2, NF, 8, cells), jnp.float32)], flops=10**9,
+        )(own, inner, jac, gradient)
 
     def exchange(own, other):
         combined = kernel_call(
@@ -175,20 +182,21 @@
         )(own, other)
         return lax.all_to_all(combined, "tm", 0, 0, tiled=True, axis_index_groups=groups)
 
-    def no_swap(near):
-        return jnp.zeros((2, *near.shape), near.dtype)
-
-    def in_turn(own, other, near, swapped):
-        return exchange(own, other), swapped
-
-    def together(own, other, near, swapped):
-        return exchange(own, other), swap(near)
-
-    part = kernel_call(
-        along_kernel, "along", field, [VMEM] * 4, [pltpu.VMEM((2, NF, 8, cells), jnp.float32)],
-    )(own, inner, jac_local[0], objective_gradient[0])
-    swapped = lax.cond(late, swap, no_swap, near)
-    spectral, near = lax.cond(late, in_turn, together, own, other, near, swapped)
+    def before(near, *local):
+        return swap(near), along(*local)
+
+    def not_yet(near, *local):
+        return jnp.zeros((2, *near.shape), near.dtype), jnp.zeros_like(own)
+
+    def in_turn(own, other, near, swapped, part, *local):
+        return exchange(own, other), swapped, part
+
+    def together(own, other, near, swapped, part, *local):
+        return exchange(own, other), swap(near), along(*local)
+
+    local = (own, inner, jac_local[0], objective_gradient[0])
+    swapped, part = lax.cond(late, before, not_yet, near, *local)
+    spectral, near, part = lax.cond(late, in_turn, together, own, other, near, swapped, part, *local)
     out = kernel_call(
         faces_kernel, "faces", field, [VMEM] * 7,
         [

time: 26.2 us -> 26 us (level)
  waiting for transfers between devices: 4.03 us -> 3.73 us
    all_to_all x1, waiting for transfers between devices: 4.03 us -> 3.73 us  [exchange(): lax.all_to_all(combined, 'tm', 0, 0, tiled=True, axis_index_groups=groups)]
where the time goes in v5:
time: 26 us; the launch traced here: 25.8 us
  starting transfers between devices  17.3 us (67%)
  waiting for transfers between devices  3.73 us (14%)
  Pallas kernels  2.61 us (10%)
  blocking collectives  1.85 us (7%)
    ppermute x1, starting transfers between devices, body(): lax.ppermute(far, 'space', [pair for i in range(1, count - 1, 2) for pair...  8.41 us
    ppermute x1, starting transfers between devices, body(): other = lax.ppermute(adjoint[0], 'tm', [(i, i ^ 1) for i in range(NT)])  4.88 us
    all_to_all x1, starting transfers between devices, exchange(): lax.all_to_all(combined, 'tm', 0, 0, tiled=True, axis_index_groups=groups)  4.01 us
    all_to_all x1, waiting for transfers between devices, exchange(): lax.all_to_all(combined, 'tm', 0, 0, tiled=True, axis_index_groups=groups)  3.73 us
    all_gather x1, blocking collectives, swap(): return lax.all_gather(near, 'space', axis=0, axis_index_groups=pairs)  1.85 us
    pallas_call x1, Pallas kernels, body(): kernel_call(faces_kernel, 'faces', field, [VMEM] * 7, [pltpu.VMEM(((NF +...  1 us
    pallas_call x1, Pallas kernels, exchange(): kernel_call(combine_kernel, 'combine', jax.ShapeDtypeStruct((PAIRS, NF, l...  0.79 us
    pallas_call x1, Pallas kernels, body(): kernel_call(across_kernel, 'across', (field, face, face), [VMEM] * 3, [pl...  0.52 us
  transfers between devices with their start and end apart: 3, of which 1 were waited for; matrix products, arithmetic and copies ran while one was open for 0% of the time, Pallas kernels for 6%

profile of v5, /device:TPU:217, one launch (start us, length us, event | category | flops | bytes accessed | tf_op | source)
XLA Modules:
  0.0 25.8 jit_solution(5008028140251317229)
XLA Ops:
  0.0 0.0 copy-start
  0.0 0.0 copy-start.4
  0.0 4.9 %collective-permute-start = (f32[5,4,1024]{2,1,0:T(4,128)}, f32[5,4,1024]{2,1,0:T(4,128)S(1)}, u32[]{:S(2)}, u32[]{:S(2)}) collective-permute-start(f32[5,4,1024]{2,1,0:T(4,128)} %bitcast.8), channel_id=1, source_target_pairs={{0,64},{64,0},{128,192},{192,128},{256,320},{320,256},{384,448},{4... | collective-permute-start | bytes 245768 | tf_op jit(solution)/shard_map/ppermute | solution.py:156
  4.9 0.0 copy-start.5
  4.9 0.0 copy-start.6
  4.9 0.0 copy-done
  4.9 0.0 copy-done.4
  4.9 0.5 %across.1 = (f32[5,4,1024]{2,1,0:T(4,128)S(1)}, f32[5,2,1024]{2,1,0:T(2,128)S(1)}, f32[5,2,1024]{2,1,0:T(2,128)S(1)}) custom-call(f32[8,128]{1,0:T(8,128)S(1)} %zeros.1.zeros_ref, f32[5,4,1024]{2,1,0:T(4,128)S(1)} %bitcast.9, f32[4,5,5,4,1024]{4,3,2,1,0:T(4,128)S(1)} %bitcast.7), custom_call_target="tpu_custom_call" | custom-call | flops 819200 | bytes 1720320 | tf_op jit(solution)/shard_map/across/pallas_call | solution.py:159
  5.5 8.4 %collective-permute-start.1 = (f32[5,2,1024]{2,1,0:T(2,128)S(1)}, f32[5,2,1024]{2,1,0:T(2,128)S(1)}, u32[]{:S(2)}, u32[]{:S(2)}) collective-permute-start(f32[5,2,1024]{2,1,0:T(2,128)S(1)} %get-tuple-element.65), channel_id=1, source_target_pairs={{1,2},{2,1},{3,4},{4,3},{5,6},{6,5},{7,8},{8,7},{9,10},{10,9},{11,... | collective-permute-start | bytes 122888 | tf_op jit(solution)/shard_map/ppermute | solution.py:163
  13.9 0.0 copy-done.5
  13.9 0.0 copy-done.6
  13.9 0.1 conditional.2
  14.0 0.0 collective-permute-done
  14.0 0.0 copy-start.1
  14.0 0.0 copy-start.2
  14.0 0.0 copy-start.3
  14.0 10.7 %conditional.3 = (f32[4,5,4,1024]{3,2,1,0:T(4,128)S(1)}, f32[2,5,2,1024]{3,2,1,0:T(2,128)S(1)}, f32[5,4,1024]{2,1,0:T(4,128)S(1)}) conditional(s32[]{:T(128)} %convert_element_type.4, (f32[5,4,1024]{2,1,0:T(4,128)S(1)}, f32[5,4,1024]{2,1,0:T(4,128)S(1)}, f32[5,2,1024]{2,1,0:T(2,128)S(1)}, f32[5,4,1024]{2,1,0:T(4,128)S(1)}, ...), branch_computations={%region_2.3_spmd, %region_3.4_spmd} | conditional | flops 1000245760 | bytes 1597496 | solution.py:199
  14.1 0.8 %combine.2 = f32[4,5,4,1024]{3,2,1,0:T(4,128)} custom-call(f32[5,4,1024]{2,1,0:T(4,128)S(1)} %get-tuple-element.40.own_ref, f32[5,4,1024]{2,1,0:T(4,128)S(1)} %get-tuple-element.41.other_ref), custom_call_target="tpu_custom_call" | custom-call | flops 245760 | bytes 491520 | tf_op jit(solution)/shard_map/cond/branch_0_fun/combine/pallas_call | solution.py:179
  14.8 4.0 %all-to-all-start = ((f32[4,5,4,1024]{3,2,1,0:T(4,128)}), f32[4,5,4,1024]{3,2,1,0:T(4,128)S(1)}, u32[]{:S(2)}, u32[]{:S(2)}) async-start(f32[4,5,4,1024]{3,2,1,0:T(4,128)} %combine.2), calls=%async_computation | async-start | bytes 655360 | tf_op jit(solution)/shard_map/cond/branch_0_fun/all_to_all | solution.py:183
  18.9 1.9 %all-gather.1 = f32[10,2,1024]{2,1,0:T(2,128)S(1)} all-gather(f32[5,2,1024]{2,1,0:T(2,128)S(1)} %get-tuple-element.42), channel_id=3, replica_groups={{0,1},{2,3},{4,5},{6,7},{8,9},{10,11},{12,13},{14,15},{16,17},{18,19},{..., dimensions={0}, use_global_device_ids=true | all-gather | bytes 122880 | tf_op jit(solution)/shard_map/cond/branch_0_fun/all_gather | solution.py:171
  20.7 0.3 %along.3 = f32[5,4,1024]{2,1,0:T(4,128)S(1)} custom-call(f32[5,4,1024]{2,1,0:T(4,128)S(1)} %get-tuple-element.40.own_ref, f32[5,4,1024]{2,1,0:T(4,128)S(1)} %get-tuple-element.43.inner_ref, f32[3,5,5,4,1024]{4,3,2,1,0:T(4,128)S(1)} %get-tuple-element.44.jac_ref, f32[5,4,1024]{2,1,0:T(4,128)S(1)} %get-tuple-element.45.obj_ref), custom_call_target="tpu_custom_call" | custom-call | flops 1000000000 | tf_op jit(solution)/shard_map/cond/branch_0_fun/along/pallas_call | solution.py:174
  21.0 3.7 %all-to-all-done = f32[4,5,4,1024]{3,2,1,0:T(4,128)S(1)} async-done(((f32[4,5,4,1024]{3,2,1,0:T(4,128)}), f32[4,5,4,1024]{3,2,1,0:T(4,128)S(1)}, u32[]{:S(2)}, u32[]{:S(2)}) %all-to-all-start) | async-done | bytes 327712 | tf_op jit(solution)/shard_map/cond/branch_0_fun/all_to_all | solution.py:183
  24.7 0.0 collective-permute-done.1.far_ref
  24.7 0.0 copy-done.1
  24.8 0.0 copy-done.2
  24.8 0.0 copy-done.3
  24.8 1.0 %faces.1 = f32[5,4,1024]{2,1,0:T(4,128)} custom-call(f32[5,4,1024]{2,1,0:T(4,128)S(1)} %get-tuple-element.62.part_ref, f32[4,5,4,1024]{3,2,1,0:T(4,128)S(1)} %get-tuple-element.63.spec_ref, f32[4,1024]{1,0:T(4,128)S(1)} %copy-done.1, f32[2,5,2,1024]{3,2,1,0:T(2,128)S(1)} %get-tuple-element.64.near_ref, f32[5,2,1024]{2,1,0:T(2,128)S(1)} %collective-permute-done.1.far_ref, ...), custom_call_target="tpu_custom_call" | custom-call | flops 409600 | bytes 409600 | tf_op jit(solution)/shard_map/faces/pallas_call | solution.py:200
  (3 shorter events, 0.0 us)
Async XLA Ops:
  0.0 4.9 %copy-start = (f32[1,4,5,5,4,1024]{5,4,3,2,1,0:T(4,128)S(1)}, f32[1,4,5,5,4,1024]{5,4,3,2,1,0:T(4,128)}, u32[]{:S(2)}) copy-start(f32[1,4,5,5,4,1024]{5,4,3,2,1,0:T(4,128)} %param.12) | copy-start | bytes 4915204
  0.0 4.9 %copy-start.4 = (f32[1,5,4,1024]{3,2,1,0:T(4,128)S(1)}, f32[1,5,4,1024]{3,2,1,0:T(4,128)}, u32[]{:S(2)}) copy-start(f32[1,5,4,1024]{3,2,1,0:T(4,128)} %param.11) | copy-start | bytes 245764
  0.0 14.0 %collective-permute-start = (f32[5,4,1024]{2,1,0:T(4,128)}, f32[5,4,1024]{2,1,0:T(4,128)S(1)}, u32[]{:S(2)}, u32[]{:S(2)}) collective-permute-start(f32[5,4,1024]{2,1,0:T(4,128)} %bitcast.8), channel_id=1, source_target_pairs={{0,64},{64,0},{128,192},{192,128},{256,320},{320,256},{384,448},{4... | collective-permute-start | bytes 245768 | tf_op jit(solution)/shard_map/ppermute | solution.py:156
  4.9 9.0 %copy-start.5 = (f32[1,3,5,5,4,1024]{5,4,3,2,1,0:T(4,128)S(1)}, f32[1,3,5,5,4,1024]{5,4,3,2,1,0:T(4,128)}, u32[]{:S(2)}) copy-start(f32[1,3,5,5,4,1024]{5,4,3,2,1,0:T(4,128)} %param.13) | copy-start | bytes 3686404
  4.9 9.0 %copy-start.6 = (f32[1,5,4,1024]{3,2,1,0:T(4,128)S(1)}, f32[1,5,4,1024]{3,2,1,0:T(4,128)}, u32[]{:S(2)}) copy-start(f32[1,5,4,1024]{3,2,1,0:T(4,128)} %param.14) | copy-start | bytes 245764
  5.5 19.3 %collective-permute-start.1 = (f32[5,2,1024]{2,1,0:T(2,128)S(1)}, f32[5,2,1024]{2,1,0:T(2,128)S(1)}, u32[]{:S(2)}, u32[]{:S(2)}) collective-permute-start(f32[5,2,1024]{2,1,0:T(2,128)S(1)} %get-tuple-element.65), channel_id=1, source_target_pairs={{1,2},{2,1},{3,4},{4,3},{5,6},{6,5},{7,8},{8,7},{9,10},{10,9},{11,... | collective-permute-start | bytes 122888 | tf_op jit(solution)/shard_map/ppermute | solution.py:163
  14.0 10.7 %copy-start.1 = (f32[4,1024]{1,0:T(4,128)S(1)}, f32[4,1024]{1,0:T(4,128)}, u32[]{:S(2)}) copy-start(f32[4,1024]{1,0:T(4,128)} %vol_ref.1) | copy-start | bytes 49156
  14.0 10.7 %copy-start.2 = (s32[1,1024]{1,0:T(1,128)S(1)}, s32[1,1024]{1,0:T(1,128)}, u32[]{:S(2)}) copy-start(s32[1,1024]{1,0:T(1,128)} %low_ref.1) | copy-start | bytes 12292
  14.0 10.7 %copy-start.3 = (s32[1,1024]{1,0:T(1,128)S(1)}, s32[1,1024]{1,0:T(1,128)}, u32[]{:S(2)}) copy-start(s32[1,1024]{1,0:T(1,128)} %up_ref.1) | copy-start | bytes 12292
  14.8 9.9 %all-to-all-start = ((f32[4,5,4,1024]{3,2,1,0:T(4,128)}), f32[4,5,4,1024]{3,2,1,0:T(4,128)S(1)}, u32[]{:S(2)}, u32[]{:S(2)}) async-start(f32[4,5,4,1024]{3,2,1,0:T(4,128)} %combine.2), calls=%async_computation | async-start | bytes 655360 | tf_op jit(solution)/shard_map/cond/branch_0_fun/all_to_all | solution.py:183

commit v6 on v4

v6 whole, which is shorter than its diff:
```python
import jax
import jax.numpy as jnp
import numpy as np
from jax import lax
from jax.experimental import pallas as pl
from jax.experimental.pallas import tpu as pltpu
from jax.sharding import PartitionSpec as P

NT = 8
NF = 5
PAIRS = NT // 2
VMEM = pl.BlockSpec(memory_space=pltpu.VMEM)


def spectral_table(count):
    index = np.arange(count)
    offset = index[:, None] - index[None, :]
    parity = np.where(offset % 2 == 0, 1.0, -1.0)
    mask = np.logical_and(offset != 0, np.abs(offset) * 2 != count)
    safe = np.where(mask, offset, 1)
    first = np.where(mask, 0.5 * parity / np.tan(np.pi * safe / count), 0.0)
    apart = offset != 0
    wide = np.where(apart, offset, 1)
    sine = np.sin(np.pi * wide / count)
    second = np.where(apart, -0.5 * parity / (sine * sine), -(count * count + 2) / 12.0)
    return (first + 0.25 * second).astype(np.float32)


def products(fields, blocks, first, b, here):
    total = blocks[first, b, here] * fields[0]
    for a in range(1, NF):
        total = total + blocks[first + a, b, here] * fields[a]
    return total


def zeros_kernel(out_ref):
    out_ref[...] = jnp.zeros_like(out_ref)


def across_kernel(zeros_ref, own_ref, jac_ref, inner_ref, near_ref, far_ref):
    layer = lax.broadcasted_iota(jnp.int32, (8, 128), 0) % 4
    even = lax.axis_index("space") % 2 == 0

    def swapped(rows):
        return jnp.where(layer < 2, pltpu.roll(rows, 6, 0), pltpu.roll(rows, 2, 0))

    for at in range(0, own_ref.shape[1], 8):
        here = slice(at, at + 8)
        fields = [own_ref[a, here, :] for a in range(NF)]
        for b in range(NF):
            up, down, up_2, down_2 = (products(fields, jac_ref, NF * k, b, here) for k in range(4))
            inner = zeros_ref[...] + swapped(jnp.where(layer < 2, up_2, down_2))
            inner = inner + jnp.where(layer >= 1, pltpu.roll(up, 1, 0), 0.0)
            inner = inner + jnp.where(layer <= 2, pltpu.roll(down, 7, 0), 0.0)
            outer = swapped(jnp.where(layer < 2, down_2, up_2))
            outer = outer + jnp.where(layer == 0, pltpu.roll(up, 5, 0), 0.0)
            outer = outer + jnp.where(layer == 3, pltpu.roll(down, 3, 0), 0.0)
            outer = jnp.where(even, outer, swapped(outer))
            inner_ref[b, here, :] = inner
            for half in range(2):
                cells = slice(32 * at + 128 * half, 32 * at + 128 * (half + 1))
                near_ref[b, :, cells] = outer[4 * half:4 * half + 2]
                far_ref[b, :, cells] = outer[4 * half + 2:4 * half + 4]


def read_through(face, index, packed, spread):
    cells = index.shape[1]
    chunks = cells // 128
    row = lax.broadcasted_iota(jnp.int32, (8, 128), 0)
    for b in range(NF - 1):
        packed[0, 2 * b:2 * b + 2, :] = face(b)
    for copy in range(4):
        packed[1, 2 * copy:2 * copy + 2, :] = face(NF - 1)

    def look_up(group, index):
        lane, chunk = index % 128, index // 128
        total = None
        for c in range(chunks):
            piece = jnp.take_along_axis(packed[group, :, 128 * c:128 * (c + 1)], lane, axis=1, mode="promise_in_bounds")
            total = piece if c == 0 else jnp.where(chunk == c, piece, total)
        return total

    wide = [jnp.broadcast_to(index[0:1, 128 * j:128 * (j + 1)], (8, 128)) for j in range(chunks)]
    for j in range(chunks):
        spread[0, :, 128 * j:128 * (j + 1)] = look_up(0, wide[j])
    for start in range(0, chunks, 4):
        mixed = wide[start]
        for copy in range(1, 4):
            mixed = jnp.where(row // 2 == copy, wide[start + copy], mixed)
        total = look_up(1, mixed)
        for copy in range(4):
            spread[1, 0:2, 128 * (start + copy):128 * (start + copy + 1)] = total[2 * copy:2 * copy + 2]
    return [spread[b // 4, 2 * (b % 4):2 * (b % 4) + 2, :] for b in range(NF)]


def add_rows(is_lower, pieces, into):
    @pl.when(is_lower)
    def _():
        for b in range(NF):
            into[b, 0:2, :] += pieces[b]

    @pl.when(jnp.logical_not(is_lower))
    def _():
        for b in range(NF):
            into[b, 2:4, :] += pieces[b]


def along_kernel(own_ref, inner_ref, jac_ref, obj_ref, near_ref, low_ref, up_ref, part_ref, packed, spread):
    groups = range(0, own_ref.shape[1], 8)
    row = lax.broadcasted_iota(jnp.int32, (8, 128), 0)
    lane = lax.broadcasted_iota(jnp.int32, (8, 128), 1)
    nothing = jnp.zeros((8, 128), jnp.float32)
    for b in range(NF):
        center, plus, minus = [], [], []
        for at in groups:
            here = slice(at, at + 8)
            fields = [own_ref[a, here, :] for a in range(NF)]
            center.append(obj_ref[b, here, :] + inner_ref[b, here, :] + products(fields, jac_ref, 0, b, here))
            plus.append(pltpu.roll(products(fields, jac_ref, NF, b, here), 1, 1))
            minus.append(pltpu.roll(products(fields, jac_ref, 2 * NF, b, here), 127, 1))
        across_plus = [nothing] + [pltpu.roll(rows, 4, 0) for rows in plus]
        across_minus = [pltpu.roll(rows, 4, 0) for rows in minus] + [nothing]
        for i, at in enumerate(groups):
            entering = jnp.where(row < 4, across_plus[i], across_plus[i + 1])
            total = center[i] + jnp.where(lane == 0, entering, plus[i])
            entering = jnp.where(row < 4, across_minus[i], across_minus[i + 1])
            total = total + jnp.where(lane == 127, entering, minus[i])
            for half in range(2):
                part_ref[b, :, 32 * at + 128 * half:32 * at + 128 * (half + 1)] = total[4 * half:4 * half + 4]
    odd = lax.axis_index("space") % 2 == 1
    sibling = 1 - lax.axis_index("space") % 2
    index = jnp.where(odd, low_ref[...], up_ref[...])
    add_rows(odd, read_through(lambda b: near_ref[sibling, b], index, packed, spread), part_ref)


def combine_kernel(own_ref, other_ref, out_ref):
    at = lax.axis_index("tm")
    odd = at % 2 == 1
    table = spectral_table(NT)
    for j in range(PAIRS):
        ours = float(table[0, 2 * j])
        theirs = jnp.where(odd, float(table[0, (2 * j + 1) % NT]), float(table[1, 2 * j]))
        out_ref[(at // 2 + j) % PAIRS] = ours * own_ref[...] + theirs * other_ref[...]


def finish_kernel(part_ref, spec_ref, vol_ref, far_ref, low_ref, up_ref, out_ref, packed, spread):
    scale = 1.5 * vol_ref[...]
    for b in range(NF):
        spectral = spec_ref[0, b]
        for j in range(1, PAIRS):
            spectral = spectral + spec_ref[j, b]
        out_ref[b] = part_ref[b] + scale * spectral
    space = lax.axis_index("space")

    @pl.when(jnp.logical_and(space > 0, space < lax.axis_size("space") - 1))
    def _():
        even = space % 2 == 0
        index = jnp.where(even, low_ref[...], up_ref[...])
        add_rows(even, read_through(lambda b: far_ref[b], index, packed, spread), out_ref)


def by_rows(array):
    *lead, layers, cells = array.shape
    split = array.reshape(-1, layers, cells // 128, 128).transpose(0, 2, 1, 3)
    return split.reshape(-1, layers * cells // 128, 128)


def kernel_call(kernel, name, out_shape, in_specs, scratch=(), out_specs=None, limit=2**20, flops=0, moved=0):
    if out_specs is None:
        out_specs = jax.tree.map(lambda _: VMEM, out_shape)
    return pl.pallas_call(
        kernel,
        out_shape=out_shape,
        in_specs=in_specs,
        out_specs=out_specs,
        scratch_shapes=scratch,
        cost_estimate=pl.CostEstimate(flops=flops, bytes_accessed=moved, transcendentals=0),
        compiler_params=pltpu.CompilerParams(vmem_limit_bytes=limit),
        name=name,
    )


def body(adjoint, jac_x, jac_local, objective_gradient, volume, face_lower, face_upper):
    _, _, layers, cells = adjoint.shape
    count = lax.axis_size("space")
    block = NF * layers * cells
    field = jax.ShapeDtypeStruct((NF, layers, cells), jnp.float32)
    face = jax.ShapeDtypeStruct((NF, 2, cells), jnp.float32)
    other = lax.ppermute(adjoint[0], "tm", [(i, i ^ 1) for i in range(NT)])
    rows = jax.ShapeDtypeStruct((NF, layers * cells // 128, 128), jnp.float32)
    zeros = kernel_call(zeros_kernel, "zeros", jax.ShapeDtypeStruct((8, 128), jnp.float32), [], flops=10**11)()
    own = adjoint[0]
    inner, near, far = kernel_call(
        across_kernel, "across", (rows, face, face), [VMEM] * 3, flops=40 * block, moved=84 * block,
    )(zeros, by_rows(own), by_rows(jac_x[0]).reshape(4 * NF, NF, -1, 128))
    far = lax.ppermute(far, "space", [pair for i in range(1, count - 1, 2) for pair in ((i, i + 1), (i + 1, i))])
    groups = [list(range(parity, NT, 2)) for parity in range(2)]
    pairs = [[i, i + 1] for i in range(0, count, 2)]
    gathering = [pltpu.VMEM((2, 8, cells), jnp.float32)] * 2

    def along(own, inner, near, jac, gradient, low, up):
        near = lax.all_gather(near, "space", axis=0, axis_index_groups=pairs)
        return kernel_call(
            along_kernel, "along", field, [VMEM] * 7, gathering, flops=10**9,
        )(by_rows(own), inner, by_rows(jac).reshape(3 * NF, NF, -1, 128), by_rows(gradient), near, low, up)

    def exchange(own, other):
        combined = kernel_call(
            combine_kernel, "combine", jax.ShapeDtypeStruct((PAIRS, NF, layers, cells), jnp.float32), [VMEM] * 2,
            flops=12 * block, moved=24 * block,
        )(own, other)
        return lax.all_to_all(combined, "tm", 0, 0, tiled=True, axis_index_groups=groups)

    def not_yet(*local):
        return jnp.zeros_like(own)

    def in_turn(own, other, part, *local):
        return exchange(own, other), part

    def together(own, other, part, *local):
        return exchange(own, other), along(*local)

    space = lax.axis_index("space")
    edge = jnp.logical_and(space >= 2, jnp.logical_or(space % 8 < 2, space % 8 >= 6))
    middle = jnp.logical_and(space // 8 == count // 16 - 1, space % 8 >= 6)
    edge = jnp.logical_and(edge, jnp.logical_or(lax.axis_index("tm") % 2 == 0, middle))
    local = (own, inner, near, jac_local[0], objective_gradient[0], face_lower, face_upper)
    part = lax.cond(jnp.logical_not(edge), along, not_yet, *local)
    spectral, part = lax.cond(jnp.logical_not(edge), in_turn, together, own, other, part, *local)
    out = kernel_call(
        finish_kernel, "finish", field, [VMEM] * 6, gathering, flops=20 * block, moved=20 * block,
    )(part, spectral, volume, far, face_lower, face_upper)
    return out[None]


def solution(mesh):
    in_specs = (
        P("tm", None, "space", None),
        P("tm", None, None, None, "space", None),
        P("tm", None, None, None, "space", None),
        P("tm", None, "space", None),
        P("space", None),
        P("space", None),
        P("space", None),
    )
    out_specs = P("tm", None, "space", None)
    return jax.shard_map(body, mesh=mesh, in_specs=in_specs, out_specs=out_specs, check_vma=False)
```

time: 26.2 us -> 25.7 us (0.981)
  Pallas kernels: 2.59 us -> 2.2 us
  waiting for transfers between devices: 4.03 us -> 3.73 us
    pallas_call x3, Pallas kernels: 1.81 us -> 1.41 us  [the longest x1 0.89 us: body(): kernel_call(finish_kernel, 'finish', field, [VMEM] * 6, gathering, flops=...]
    all_to_all x1, waiting for transfers between devices: 4.03 us -> 3.72 us  [exchange(): lax.all_to_all(combined, 'tm', 0, 0, tiled=True, axis_index_groups=groups)]
  transfers between devices with their start and end apart: 3 -> 3, of which waited for: 1 -> 1; matrix products, arithmetic and copies ran while one was open for 0% -> 0% of each run, Pallas kernels for 6% -> 5%
where the time goes in v6:
time: 25.7 us; the launch traced here: 25.5 us
  starting transfers between devices  17.4 us (68%)
  waiting for transfers between devices  3.73 us (15%)
  Pallas kernels  2.2 us (9%)
  blocking collectives  1.85 us (7%)
    ppermute x1, starting transfers between devices, body(): lax.ppermute(far, 'space', [pair for i in range(1, count - 1, 2) for pair...  8.54 us
    ppermute x1, starting transfers between devices, body(): other = lax.ppermute(adjoint[0], 'tm', [(i, i ^ 1) for i in range(NT)])  4.88 us
    all_to_all x1, starting transfers between devices, exchange(): lax.all_to_all(combined, 'tm', 0, 0, tiled=True, axis_index_groups=groups)  4.01 us
    all_to_all x1, waiting for transfers between devices, exchange(): lax.all_to_all(combined, 'tm', 0, 0, tiled=True, axis_index_groups=groups)  3.72 us
    all_gather x1, blocking collectives, along(): near = lax.all_gather(near, 'space', axis=0, axis_index_groups=pairs)  1.85 us
    pallas_call x1, Pallas kernels, body(): kernel_call(finish_kernel, 'finish', field, [VMEM] * 6, gathering, flops=...  0.89 us
    pallas_call x1, Pallas kernels, exchange(): kernel_call(combine_kernel, 'combine', jax.ShapeDtypeStruct((PAIRS, NF, l...  0.79 us
  transfers between devices with their start and end apart: 3, of which 1 were waited for; matrix products, arithmetic and copies ran while one was open for 0% of the time, Pallas kernels for 5%

profile of v6, /device:TPU:217, one launch (start us, length us, event | category | flops | bytes accessed | tf_op | source)
XLA Modules:
  0.0 25.5 jit_solution(6205624780835463014)
XLA Ops:
  0.0 0.0 copy-start
  0.0 0.0 copy-start.2
  0.0 4.9 %collective-permute-start = (f32[5,4,1024]{2,1,0:T(4,128)}, f32[5,4,1024]{2,1,0:T(4,128)S(1)}, u32[]{:S(2)}, u32[]{:S(2)}) collective-permute-start(f32[5,4,1024]{2,1,0:T(4,128)} %bitcast.47), channel_id=1, source_target_pairs={{0,64},{64,0},{128,192},{192,128},{256,320},{320,256},{384,448},{4... | collective-permute-start | bytes 245768 | tf_op jit(solution)/shard_map/ppermute | solution.py:189
  4.9 0.0 copy-start.3
  4.9 0.0 copy-start.4
  4.9 0.0 copy-start.5
  4.9 0.0 copy-start.6
  4.9 0.0 copy-done
  5.0 0.0 copy-done.2
  5.0 0.2 across.1
  5.2 8.5 %collective-permute-start.1 = (f32[5,2,1024]{2,1,0:T(2,128)S(1)}, f32[5,2,1024]{2,1,0:T(2,128)S(1)}, u32[]{:S(2)}, u32[]{:S(2)}) collective-permute-start(f32[5,2,1024]{2,1,0:T(2,128)S(1)} %get-tuple-element.74), channel_id=1, source_target_pairs={{1,2},{2,1},{3,4},{4,3},{5,6},{6,5},{7,8},{8,7},{9,10},{10,9},{11,... | collective-permute-start | bytes 122888 | tf_op jit(solution)/shard_map/ppermute | solution.py:196
  13.8 0.0 copy-done.3
  13.8 0.0 copy-done.4
  13.8 0.0 copy-done.5
  13.8 0.0 copy-done.6
  13.9 0.0 collective-permute-done
  13.9 0.0 copy-start.1
  13.9 10.7 %conditional.3 = (f32[4,5,4,1024]{3,2,1,0:T(4,128)S(1)}, f32[5,4,1024]{2,1,0:T(4,128)S(1)}) conditional(s32[]{:T(128)} %convert_element_type.4, (f32[5,4,1024]{2,1,0:T(4,128)S(1)}, f32[5,4,1024]{2,1,0:T(4,128)S(1)}, f32[1,5,4,1024]{3,2,1,0:T(4,128)S(1)}, f32[1,3,5,5,4,1024]{5,4,3,2,1,0:T(4,128)S(1)}, f32[1,5,4,1024]{3,2,1,0:T(4,128)S(1)}, ...), branch_computations={%region_2.3_spmd, %region_3.4_spmd} | conditional | flops 1000245760 | bytes 1597488 | solution.py:229
  13.9 0.8 %combine.2 = f32[4,5,4,1024]{3,2,1,0:T(4,128)} custom-call(f32[5,4,1024]{2,1,0:T(4,128)S(1)} %bitcast.52, f32[5,4,1024]{2,1,0:T(4,128)S(1)} %get-tuple-element.54.other_ref), custom_call_target="tpu_custom_call" | custom-call | flops 245760 | bytes 491520 | tf_op jit(solution)/shard_map/cond/branch_0_fun/combine/pallas_call | solution.py:208
  14.7 4.0 %all-to-all-start = ((f32[4,5,4,1024]{3,2,1,0:T(4,128)}), f32[4,5,4,1024]{3,2,1,0:T(4,128)S(1)}, u32[]{:S(2)}, u32[]{:S(2)}) async-start(f32[4,5,4,1024]{3,2,1,0:T(4,128)} %combine.2), calls=%async_computation | async-start | bytes 655360 | tf_op jit(solution)/shard_map/cond/branch_0_fun/all_to_all | solution.py:212
  18.7 1.9 %all-gather.1 = f32[10,2,1024]{2,1,0:T(2,128)S(1)} all-gather(f32[5,2,1024]{2,1,0:T(2,128)S(1)} %get-tuple-element.59), channel_id=3, replica_groups={{0,1},{2,3},{4,5},{6,7},{8,9},{10,11},{12,13},{14,15},{16,17},{18,19},{..., dimensions={0}, use_global_device_ids=true | all-gather | bytes 122880 | tf_op jit(solution)/shard_map/cond/branch_0_fun/all_gather | solution.py:202
  20.6 0.3 %along.3 = f32[5,4,1024]{2,1,0:T(4,128)S(1)} custom-call(f32[5,32,128]{2,1,0:T(8,128)S(1)} %bitcast.53, f32[5,32,128]{2,1,0:T(8,128)S(1)} %get-tuple-element.56.inner_ref, f32[15,5,32,128]{3,2,1,0:T(8,128)S(1)} %bitcast.55, f32[5,32,128]{2,1,0:T(8,128)S(1)} %bitcast.57, f32[2,5,2,1024]{3,2,1,0:T(2,128)S(1)} %bitcast.45, ...), custom_call_target="tpu_custom_call" | custom-call | flops 1000000000 | tf_op jit(solution)/shard_map/cond/branch_0_fun/along/pallas_call | solution.py:203
  20.9 3.7 %all-to-all-done = f32[4,5,4,1024]{3,2,1,0:T(4,128)S(1)} async-done(((f32[4,5,4,1024]{3,2,1,0:T(4,128)}), f32[4,5,4,1024]{3,2,1,0:T(4,128)S(1)}, u32[]{:S(2)}, u32[]{:S(2)}) %all-to-all-start) | async-done | bytes 327712 | tf_op jit(solution)/shard_map/cond/branch_0_fun/all_to_all | solution.py:212
  24.6 0.0 collective-permute-done.1.far_ref
  24.6 0.0 copy-done.1
  24.6 0.9 %finish.1 = f32[5,4,1024]{2,1,0:T(4,128)} custom-call(f32[5,4,1024]{2,1,0:T(4,128)S(1)} %get-tuple-element.72.part_ref, f32[4,5,4,1024]{3,2,1,0:T(4,128)S(1)} %get-tuple-element.73.spec_ref, f32[4,1024]{1,0:T(4,128)S(1)} %copy-done.1, f32[5,2,1024]{2,1,0:T(2,128)S(1)} %collective-permute-done.1.far_ref, s32[1,1024]{1,0:T(1,128)S(1)} %copy-done.3, ...), custom_call_target="tpu_custom_call" | custom-call | flops 409600 | bytes 409600 | tf_op jit(solution)/shard_map/finish/pallas_call | solution.py:230
  (3 shorter events, 0.0 us)
Async XLA Ops:
  0.0 4.9 %copy-start = (f32[1,4,5,5,4,1024]{5,4,3,2,1,0:T(4,128)S(1)}, f32[1,4,5,5,4,1024]{5,4,3,2,1,0:T(4,128)}, u32[]{:S(2)}) copy-start(f32[1,4,5,5,4,1024]{5,4,3,2,1,0:T(4,128)} %param.12) | copy-start | bytes 4915204
  0.0 5.0 %copy-start.2 = (f32[1,5,4,1024]{3,2,1,0:T(4,128)S(1)}, f32[1,5,4,1024]{3,2,1,0:T(4,128)}, u32[]{:S(2)}) copy-start(f32[1,5,4,1024]{3,2,1,0:T(4,128)} %param.11) | copy-start | bytes 245764
  0.0 13.9 %collective-permute-start = (f32[5,4,1024]{2,1,0:T(4,128)}, f32[5,4,1024]{2,1,0:T(4,128)S(1)}, u32[]{:S(2)}, u32[]{:S(2)}) collective-permute-start(f32[5,4,1024]{2,1,0:T(4,128)} %bitcast.47), channel_id=1, source_target_pairs={{0,64},{64,0},{128,192},{192,128},{256,320},{320,256},{384,448},{4... | collective-permute-start | bytes 245768 | tf_op jit(solution)/shard_map/ppermute | solution.py:189
  4.9 8.9 %copy-start.3 = (s32[1,1024]{1,0:T(1,128)S(1)}, s32[1,1024]{1,0:T(1,128)}, u32[]{:S(2)}) copy-start(s32[1,1024]{1,0:T(1,128)} %low_ref.1) | copy-start | bytes 12292
  4.9 8.9 %copy-start.4 = (s32[1,1024]{1,0:T(1,128)S(1)}, s32[1,1024]{1,0:T(1,128)}, u32[]{:S(2)}) copy-start(s32[1,1024]{1,0:T(1,128)} %up_ref.1) | copy-start | bytes 12292
  4.9 8.9 %copy-start.5 = (f32[1,3,5,5,4,1024]{5,4,3,2,1,0:T(4,128)S(1)}, f32[1,3,5,5,4,1024]{5,4,3,2,1,0:T(4,128)}, u32[]{:S(2)}) copy-start(f32[1,3,5,5,4,1024]{5,4,3,2,1,0:T(4,128)} %param.13) | copy-start | bytes 3686404
  4.9 8.9 %copy-start.6 = (f32[1,5,4,1024]{3,2,1,0:T(4,128)S(1)}, f32[1,5,4,1024]{3,2,1,0:T(4,128)}, u32[]{:S(2)}) copy-start(f32[1,5,4,1024]{3,2,1,0:T(4,128)} %param.14) | copy-start | bytes 245764
  5.2 19.4 %collective-permute-start.1 = (f32[5,2,1024]{2,1,0:T(2,128)S(1)}, f32[5,2,1024]{2,1,0:T(2,128)S(1)}, u32[]{:S(2)}, u32[]{:S(2)}) collective-permute-start(f32[5,2,1024]{2,1,0:T(2,128)S(1)} %get-tuple-element.74), channel_id=1, source_target_pairs={{1,2},{2,1},{3,4},{4,3},{5,6},{6,5},{7,8},{8,7},{9,10},{10,9},{11,... | collective-permute-start | bytes 122888 | tf_op jit(solution)/shard_map/ppermute | solution.py:196
  13.9 10.7 %copy-start.1 = (f32[4,1024]{1,0:T(4,128)S(1)}, f32[4,1024]{1,0:T(4,128)}, u32[]{:S(2)}) copy-start(f32[4,1024]{1,0:T(4,128)} %vol_ref.1) | copy-start | bytes 49156
  14.7 9.9 %all-to-all-start = ((f32[4,5,4,1024]{3,2,1,0:T(4,128)}), f32[4,5,4,1024]{3,2,1,0:T(4,128)S(1)}, u32[]{:S(2)}, u32[]{:S(2)}) async-start(f32[4,5,4,1024]{3,2,1,0:T(4,128)} %combine.2), calls=%async_computation | async-start | bytes 655360 | tf_op jit(solution)/shard_map/cond/branch_0_fun/all_to_all | solution.py:212

commit v7 on v6

--- a/solution.py
+++ b/solution.py
@@ -9,6 +9,7 @@
 NT = 8
 NF = 5
 PAIRS = NT // 2
+ORDER = (0, 3, 1, 2)
 VMEM = pl.BlockSpec(memory_space=pltpu.VMEM)
 
 
@@ -140,7 +141,11 @@
     for j in range(PAIRS):
         ours = float(table[0, 2 * j])
         theirs = jnp.where(odd, float(table[0, (2 * j + 1) % NT]), float(table[1, 2 * j]))
-        out_ref[(at // 2 + j) % PAIRS] = ours * own_ref[...] + theirs * other_ref[...]
+        pair = (at // 2 + j) % PAIRS
+        slot = 0
+        for place, member in enumerate(ORDER):
+            slot = jnp.where(pair == member, place, slot)
+        out_ref[slot] = ours * own_ref[...] + theirs * other_ref[...]
 
 
 def finish_kernel(part_ref, spec_ref, vol_ref, far_ref, low_ref, up_ref, out_ref, packed, spread):
@@ -194,7 +199,7 @@
         across_kernel, "across", (rows, face, face), [VMEM] * 3, flops=40 * block, moved=84 * block,
     )(zeros, by_rows(own), by_rows(jac_x[0]).reshape(4 * NF, NF, -1, 128))
     far = lax.ppermute(far, "space", [pair for i in range(1, count - 1, 2) for pair in ((i, i + 1), (i + 1, i))])
-    groups = [list(range(parity, NT, 2)) for parity in range(2)]
+    groups = [[2 * pair + parity for pair in ORDER] for parity in range(2)]
     pairs = [[i, i + 1] for i in range(0, count, 2)]
     gathering = [pltpu.VMEM((2, 8, cells), jnp.float32)] * 2
 

time: 25.7 us -> 25.4 us (0.988)
  waiting for transfers between devices: 3.73 us -> 3.43 us
    all_to_all x1, waiting for transfers between devices: 3.72 us -> 3.43 us  [exchange(): lax.all_to_all(combined, 'tm', 0, 0, tiled=True, axis_index_groups=groups)]
where the time goes in v7:
time: 25.4 us; the launch traced here: 25.2 us
  starting transfers between devices  17.4 us (69%)
  waiting for transfers between devices  3.43 us (14%)
  Pallas kernels  2.19 us (9%)
  blocking collectives  1.85 us (7%)
    ppermute x1, starting transfers between devices, body(): lax.ppermute(far, 'space', [pair for i in range(1, count - 1, 2) for pair...  8.54 us
    ppermute x1, starting transfers between devices, body(): other = lax.ppermute(adjoint[0], 'tm', [(i, i ^ 1) for i in range(NT)])  4.88 us
    all_to_all x1, starting transfers between devices, exchange(): lax.all_to_all(combined, 'tm', 0, 0, tiled=True, axis_index_groups=groups)  4.01 us
    all_to_all x1, waiting for transfers between devices, exchange(): lax.all_to_all(combined, 'tm', 0, 0, tiled=True, axis_index_groups=groups)  3.43 us
    all_gather x1, blocking collectives, along(): near = lax.all_gather(near, 'space', axis=0, axis_index_groups=pairs)  1.85 us
    pallas_call x1, Pallas kernels, body(): kernel_call(finish_kernel, 'finish', field, [VMEM] * 6, gathering, flops=...  0.89 us
    pallas_call x1, Pallas kernels, exchange(): kernel_call(combine_kernel, 'combine', jax.ShapeDtypeStruct((PAIRS, NF, l...  0.78 us
  transfers between devices with their start and end apart: 3, of which 1 were waited for; matrix products, arithmetic and copies ran while one was open for 0% of the time, Pallas kernels for 5%

profile of v7, /device:TPU:217, one launch (start us, length us, event | category | flops | bytes accessed | tf_op | source)
XLA Modules:
  0.0 25.2 jit_solution(12420699830378188200)
XLA Ops:
  0.0 0.0 copy-start
  0.0 0.0 copy-start.2
  0.0 4.9 %collective-permute-start = (f32[5,4,1024]{2,1,0:T(4,128)}, f32[5,4,1024]{2,1,0:T(4,128)S(1)}, u32[]{:S(2)}, u32[]{:S(2)}) collective-permute-start(f32[5,4,1024]{2,1,0:T(4,128)} %bitcast.47), channel_id=1, source_target_pairs={{0,64},{64,0},{128,192},{192,128},{256,320},{320,256},{384,448},{4... | collective-permute-start | bytes 245768 | tf_op jit(solution)/shard_map/ppermute | solution.py:194
  4.9 0.0 copy-start.3
  4.9 0.0 copy-start.4
  4.9 0.0 copy-start.5
  4.9 0.0 copy-start.6
  4.9 0.0 copy-done
  5.0 0.0 copy-done.2
  5.0 0.2 across.1
  5.2 8.5 %collective-permute-start.1 = (f32[5,2,1024]{2,1,0:T(2,128)S(1)}, f32[5,2,1024]{2,1,0:T(2,128)S(1)}, u32[]{:S(2)}, u32[]{:S(2)}) collective-permute-start(f32[5,2,1024]{2,1,0:T(2,128)S(1)} %get-tuple-element.74), channel_id=1, source_target_pairs={{1,2},{2,1},{3,4},{4,3},{5,6},{6,5},{7,8},{8,7},{9,10},{10,9},{11,... | collective-permute-start | bytes 122888 | tf_op jit(solution)/shard_map/ppermute | solution.py:201
  13.8 0.0 copy-done.3
  13.8 0.0 copy-done.4
  13.8 0.0 copy-done.5
  13.8 0.0 copy-done.6
  13.9 0.0 collective-permute-done
  13.9 0.0 copy-start.1
  13.9 10.4 %conditional.3 = (f32[4,5,4,1024]{3,2,1,0:T(4,128)S(1)}, f32[5,4,1024]{2,1,0:T(4,128)S(1)}) conditional(s32[]{:T(128)} %convert_element_type.4, (f32[5,4,1024]{2,1,0:T(4,128)S(1)}, f32[5,4,1024]{2,1,0:T(4,128)S(1)}, f32[1,5,4,1024]{3,2,1,0:T(4,128)S(1)}, f32[1,3,5,5,4,1024]{5,4,3,2,1,0:T(4,128)S(1)}, f32[1,5,4,1024]{3,2,1,0:T(4,128)S(1)}, ...), branch_computations={%region_2.3_spmd, %region_3.4_spmd} | conditional | flops 1000245760 | bytes 1597488 | solution.py:234
  13.9 0.8 %combine.2 = f32[4,5,4,1024]{3,2,1,0:T(4,128)} custom-call(f32[5,4,1024]{2,1,0:T(4,128)S(1)} %bitcast.52, f32[5,4,1024]{2,1,0:T(4,128)S(1)} %get-tuple-element.54.other_ref), custom_call_target="tpu_custom_call" | custom-call | flops 245760 | bytes 491520 | tf_op jit(solution)/shard_map/cond/branch_0_fun/combine/pallas_call | solution.py:213
  14.7 4.0 %all-to-all-start = ((f32[4,5,4,1024]{3,2,1,0:T(4,128)}), f32[4,5,4,1024]{3,2,1,0:T(4,128)S(1)}, u32[]{:S(2)}, u32[]{:S(2)}) async-start(f32[4,5,4,1024]{3,2,1,0:T(4,128)} %combine.2), calls=%async_computation | async-start | bytes 655360 | tf_op jit(solution)/shard_map/cond/branch_0_fun/all_to_all | solution.py:217
  18.7 1.9 %all-gather.1 = f32[10,2,1024]{2,1,0:T(2,128)S(1)} all-gather(f32[5,2,1024]{2,1,0:T(2,128)S(1)} %get-tuple-element.59), channel_id=3, replica_groups={{0,1},{2,3},{4,5},{6,7},{8,9},{10,11},{12,13},{14,15},{16,17},{18,19},{..., dimensions={0}, use_global_device_ids=true | all-gather | bytes 122880 | tf_op jit(solution)/shard_map/cond/branch_0_fun/all_gather | solution.py:207
  20.5 0.3 %along.3 = f32[5,4,1024]{2,1,0:T(4,128)S(1)} custom-call(f32[5,32,128]{2,1,0:T(8,128)S(1)} %bitcast.53, f32[5,32,128]{2,1,0:T(8,128)S(1)} %get-tuple-element.56.inner_ref, f32[15,5,32,128]{3,2,1,0:T(8,128)S(1)} %bitcast.55, f32[5,32,128]{2,1,0:T(8,128)S(1)} %bitcast.57, f32[2,5,2,1024]{3,2,1,0:T(2,128)S(1)} %bitcast.45, ...), custom_call_target="tpu_custom_call" | custom-call | flops 1000000000 | tf_op jit(solution)/shard_map/cond/branch_0_fun/along/pallas_call | solution.py:208
  20.8 3.4 %all-to-all-done = f32[4,5,4,1024]{3,2,1,0:T(4,128)S(1)} async-done(((f32[4,5,4,1024]{3,2,1,0:T(4,128)}), f32[4,5,4,1024]{3,2,1,0:T(4,128)S(1)}, u32[]{:S(2)}, u32[]{:S(2)}) %all-to-all-start) | async-done | bytes 327712 | tf_op jit(solution)/shard_map/cond/branch_0_fun/all_to_all | solution.py:217
  24.3 0.0 collective-permute-done.1.far_ref
  24.3 0.0 copy-done.1
  24.3 0.9 %finish.1 = f32[5,4,1024]{2,1,0:T(4,128)} custom-call(f32[5,4,1024]{2,1,0:T(4,128)S(1)} %get-tuple-element.72.part_ref, f32[4,5,4,1024]{3,2,1,0:T(4,128)S(1)} %get-tuple-element.73.spec_ref, f32[4,1024]{1,0:T(4,128)S(1)} %copy-done.1, f32[5,2,1024]{2,1,0:T(2,128)S(1)} %collective-permute-done.1.far_ref, s32[1,1024]{1,0:T(1,128)S(1)} %copy-done.3, ...), custom_call_target="tpu_custom_call" | custom-call | flops 409600 | bytes 409600 | tf_op jit(solution)/shard_map/finish/pallas_call | solution.py:235
  (3 shorter events, 0.0 us)
Async XLA Ops:
  0.0 4.9 %copy-start = (f32[1,4,5,5,4,1024]{5,4,3,2,1,0:T(4,128)S(1)}, f32[1,4,5,5,4,1024]{5,4,3,2,1,0:T(4,128)}, u32[]{:S(2)}) copy-start(f32[1,4,5,5,4,1024]{5,4,3,2,1,0:T(4,128)} %param.12) | copy-start | bytes 4915204
  0.0 5.0 %copy-start.2 = (f32[1,5,4,1024]{3,2,1,0:T(4,128)S(1)}, f32[1,5,4,1024]{3,2,1,0:T(4,128)}, u32[]{:S(2)}) copy-start(f32[1,5,4,1024]{3,2,1,0:T(4,128)} %param.11) | copy-start | bytes 245764
  0.0 13.9 %collective-permute-start = (f32[5,4,1024]{2,1,0:T(4,128)}, f32[5,4,1024]{2,1,0:T(4,128)S(1)}, u32[]{:S(2)}, u32[]{:S(2)}) collective-permute-start(f32[5,4,1024]{2,1,0:T(4,128)} %bitcast.47), channel_id=1, source_target_pairs={{0,64},{64,0},{128,192},{192,128},{256,320},{320,256},{384,448},{4... | collective-permute-start | bytes 245768 | tf_op jit(solution)/shard_map/ppermute | solution.py:194
  4.9 8.9 %copy-start.3 = (s32[1,1024]{1,0:T(1,128)S(1)}, s32[1,1024]{1,0:T(1,128)}, u32[]{:S(2)}) copy-start(s32[1,1024]{1,0:T(1,128)} %low_ref.1) | copy-start | bytes 12292
  4.9 8.9 %copy-start.4 = (s32[1,1024]{1,0:T(1,128)S(1)}, s32[1,1024]{1,0:T(1,128)}, u32[]{:S(2)}) copy-start(s32[1,1024]{1,0:T(1,128)} %up_ref.1) | copy-start | bytes 12292
  4.9 8.9 %copy-start.5 = (f32[1,3,5,5,4,1024]{5,4,3,2,1,0:T(4,128)S(1)}, f32[1,3,5,5,4,1024]{5,4,3,2,1,0:T(4,128)}, u32[]{:S(2)}) copy-start(f32[1,3,5,5,4,1024]{5,4,3,2,1,0:T(4,128)} %param.13) | copy-start | bytes 3686404
  4.9 8.9 %copy-start.6 = (f32[1,5,4,1024]{3,2,1,0:T(4,128)S(1)}, f32[1,5,4,1024]{3,2,1,0:T(4,128)}, u32[]{:S(2)}) copy-start(f32[1,5,4,1024]{3,2,1,0:T(4,128)} %param.14) | copy-start | bytes 245764
  5.2 19.1 %collective-permute-start.1 = (f32[5,2,1024]{2,1,0:T(2,128)S(1)}, f32[5,2,1024]{2,1,0:T(2,128)S(1)}, u32[]{:S(2)}, u32[]{:S(2)}) collective-permute-start(f32[5,2,1024]{2,1,0:T(2,128)S(1)} %get-tuple-element.74), channel_id=1, source_target_pairs={{1,2},{2,1},{3,4},{4,3},{5,6},{6,5},{7,8},{8,7},{9,10},{10,9},{11,... | collective-permute-start | bytes 122888 | tf_op jit(solution)/shard_map/ppermute | solution.py:201
  13.9 10.4 %copy-start.1 = (f32[4,1024]{1,0:T(4,128)S(1)}, f32[4,1024]{1,0:T(4,128)}, u32[]{:S(2)}) copy-start(f32[4,1024]{1,0:T(4,128)} %vol_ref.1) | copy-start | bytes 49156
  14.7 9.6 %all-to-all-start = ((f32[4,5,4,1024]{3,2,1,0:T(4,128)}), f32[4,5,4,1024]{3,2,1,0:T(4,128)S(1)}, u32[]{:S(2)}, u32[]{:S(2)}) async-start(f32[4,5,4,1024]{3,2,1,0:T(4,128)} %combine.2), calls=%async_computation | async-start | bytes 655360 | tf_op jit(solution)/shard_map/cond/branch_0_fun/all_to_all | solution.py:217

commit v8 on v7

--- a/solution.py
+++ b/solution.py
@@ -1,3 +1,5 @@
+import functools
+
 import jax
 import jax.numpy as jnp
 import numpy as np
@@ -10,6 +12,7 @@
 NF = 5
 PAIRS = NT // 2
 ORDER = (0, 3, 1, 2)
+ORDER_BESIDE = (0, 2, 1, 3)
 VMEM = pl.BlockSpec(memory_space=pltpu.VMEM)
 
 
@@ -134,7 +137,7 @@
     add_rows(odd, read_through(lambda b: near_ref[sibling, b], index, packed, spread), part_ref)
 
 
-def combine_kernel(own_ref, other_ref, out_ref):
+def combine_kernel(order, own_ref, other_ref, out_ref):
     at = lax.axis_index("tm")
     odd = at % 2 == 1
     table = spectral_table(NT)
@@ -143,7 +146,7 @@
         theirs = jnp.where(odd, float(table[0, (2 * j + 1) % NT]), float(table[1, 2 * j]))
         pair = (at // 2 + j) % PAIRS
         slot = 0
-        for place, member in enumerate(ORDER):
+        for place, member in enumerate(order):
             slot = jnp.where(pair == member, place, slot)
         out_ref[slot] = ours * own_ref[...] + theirs * other_ref[...]
 
@@ -168,6 +171,11 @@
     *lead, layers, cells = array.shape
     split = array.reshape(-1, layers, cells // 128, 128).transpose(0, 2, 1, 3)
     return split.reshape(-1, layers * cells // 128, 128)
+
+
+def by_cells(rows, layers):
+    split = rows.reshape(rows.shape[0], -1, layers, 128).transpose(0, 2, 1, 3)
+    return split.reshape(rows.shape[0], layers, -1)
 
 
 def kernel_call(kernel, name, out_shape, in_specs, scratch=(), out_specs=None, limit=2**20, flops=0, moved=0):
@@ -199,7 +207,6 @@
         across_kernel, "across", (rows, face, face), [VMEM] * 3, flops=40 * block, moved=84 * block,
     )(zeros, by_rows(own), by_rows(jac_x[0]).reshape(4 * NF, NF, -1, 128))
     far = lax.ppermute(far, "space", [pair for i in range(1, count - 1, 2) for pair in ((i, i + 1), (i + 1, i))])
-    groups = [[2 * pair + parity for pair in ORDER] for parity in range(2)]
     pairs = [[i, i + 1] for i in range(0, count, 2)]
     gathering = [pltpu.VMEM((2, 8, cells), jnp.float32)] * 2
 
@@ -209,21 +216,24 @@
             along_kernel, "along", field, [VMEM] * 7, gathering, flops=10**9,
         )(by_rows(own), inner, by_rows(jac).reshape(3 * NF, NF, -1, 128), by_rows(gradient), near, low, up)
 
-    def exchange(own, other):
+    def exchange(order, own, other):
+        groups = [[2 * pair + parity for pair in order] for parity in range(2)]
         combined = kernel_call(
-            combine_kernel, "combine", jax.ShapeDtypeStruct((PAIRS, NF, layers, cells), jnp.float32), [VMEM] * 2,
+            functools.partial(combine_kernel, order), "combine", jax.ShapeDtypeStruct((PAIRS, NF, layers, cells), jnp.float32), [VMEM] * 2,
             flops=12 * block, moved=24 * block,
         )(own, other)
-        return lax.all_to_all(combined, "tm", 0, 0, tiled=True, axis_index_groups=groups)
+        sent = by_rows(combined).reshape(PAIRS, -1, 128)
+        got = lax.all_to_all(sent, "tm", 0, 0, tiled=True, axis_index_groups=groups)
+        return by_cells(got.reshape(PAIRS * NF, -1, 128), layers).reshape(PAIRS, NF, layers, cells)
 
     def not_yet(*local):
         return jnp.zeros_like(own)
 
     def in_turn(own, other, part, *local):
-        return exchange(own, other), part
+        return exchange(ORDER, own, other), part
 
     def together(own, other, part, *local):
-        return exchange(own, other), along(*local)
+        return exchange(ORDER_BESIDE, own, other), along(*local)
 
     space = lax.axis_index("space")
     edge = jnp.logical_and(space >= 2, jnp.logical_or(space % 8 < 2, space % 8 >= 6))

time: 25.4 us -> 25.4 us (level)
  no operation moved by 1% of the time
where the time goes in v8:
time: 25.4 us; the launch traced here: 25.2 us
  starting transfers between devices  17.4 us (69%)
  waiting for transfers between devices  3.43 us (14%)
  Pallas kernels  2.19 us (9%)
  blocking collectives  1.85 us (7%)
    ppermute x1, starting transfers between devices, body(): lax.ppermute(far, 'space', [pair for i in range(1, count - 1, 2) for pair...  8.54 us
    ppermute x1, starting transfers between devices, body(): other = lax.ppermute(adjoint[0], 'tm', [(i, i ^ 1) for i in range(NT)])  4.88 us
    all_to_all x1, starting transfers between devices, exchange(): got = lax.all_to_all(sent, 'tm', 0, 0, tiled=True, axis_index_groups=groups)  4.01 us
    all_to_all x1, waiting for transfers between devices, exchange(): got = lax.all_to_all(sent, 'tm', 0, 0, tiled=True, axis_index_groups=groups)  3.43 us
    all_gather x1, blocking collectives, along(): near = lax.all_gather(near, 'space', axis=0, axis_index_groups=pairs)  1.85 us
    pallas_call x1, Pallas kernels, body(): kernel_call(finish_kernel, 'finish', field, [VMEM] * 6, gathering, flops=...  0.89 us
    pallas_call x1, Pallas kernels, exchange(): kernel_call(functools.partial(combine_kernel, order), 'combine', jax.Shap...  0.78 us
  transfers between devices with their start and end apart: 3, of which 1 were waited for; matrix products, arithmetic and copies ran while one was open for 0% of the time, Pallas kernels for 5%

profile of v8, /device:TPU:217, one launch (start us, length us, event | category | flops | bytes accessed | tf_op | source)
XLA Modules:
  0.0 25.2 jit_solution(1349660866810932876)
XLA Ops:
  0.0 0.0 copy-start
  0.0 0.0 copy-start.2
  0.0 4.9 %collective-permute-start = (f32[5,4,1024]{2,1,0:T(4,128)}, f32[5,4,1024]{2,1,0:T(4,128)S(1)}, u32[]{:S(2)}, u32[]{:S(2)}) collective-permute-start(f32[5,4,1024]{2,1,0:T(4,128)} %bitcast.70), channel_id=1, source_target_pairs={{0,64},{64,0},{128,192},{192,128},{256,320},{320,256},{384,448},{4... | collective-permute-start | bytes 245768 | tf_op jit(solution)/shard_map/ppermute | solution.py:202
  4.9 0.0 copy-start.3
  4.9 0.0 copy-start.4
  4.9 0.0 copy-start.5
  4.9 0.0 copy-start.6
  4.9 0.0 copy-done
  5.0 0.0 copy-done.2
  5.0 0.2 across.1
  5.2 8.5 %collective-permute-start.1 = (f32[5,2,1024]{2,1,0:T(2,128)S(1)}, f32[5,2,1024]{2,1,0:T(2,128)S(1)}, u32[]{:S(2)}, u32[]{:S(2)}) collective-permute-start(f32[5,2,1024]{2,1,0:T(2,128)S(1)} %get-tuple-element.74), channel_id=1, source_target_pairs={{1,2},{2,1},{3,4},{4,3},{5,6},{6,5},{7,8},{8,7},{9,10},{10,9},{11,... | collective-permute-start | bytes 122888 | tf_op jit(solution)/shard_map/ppermute | solution.py:209
  13.8 0.0 copy-done.3
  13.8 0.0 copy-done.4
  13.8 0.0 copy-done.5
  13.8 0.0 copy-done.6
  13.9 0.0 collective-permute-done
  13.9 0.0 copy-start.1
  13.9 10.4 %conditional.3 = (f32[4,5,4,1024]{3,2,1,0:T(4,128)S(1)}, f32[5,4,1024]{2,1,0:T(4,128)S(1)}) conditional(s32[]{:T(128)} %convert_element_type.4, (f32[5,4,1024]{2,1,0:T(4,128)S(1)}, f32[5,4,1024]{2,1,0:T(4,128)S(1)}, f32[1,5,4,1024]{3,2,1,0:T(4,128)S(1)}, f32[1,3,5,5,4,1024]{5,4,3,2,1,0:T(4,128)S(1)}, f32[1,5,4,1024]{3,2,1,0:T(4,128)S(1)}, ...), branch_computations={%region_2.3_spmd, %region_3.4_spmd} | conditional | flops 1000245760 | bytes 1597488 | solution.py:244
  13.9 0.8 %combine.2 = f32[4,5,4,1024]{3,2,1,0:T(4,128)} custom-call(f32[5,4,1024]{2,1,0:T(4,128)S(1)} %bitcast.75, f32[5,4,1024]{2,1,0:T(4,128)S(1)} %get-tuple-element.54.other_ref), custom_call_target="tpu_custom_call" | custom-call | flops 245760 | bytes 491520 | tf_op jit(solution)/shard_map/cond/branch_0_fun/combine/pallas_call | solution.py:221
  14.7 4.0 %all-to-all-start = ((f32[4,160,128]{2,1,0:T(8,128)}), f32[4,160,128]{2,1,0:T(8,128)S(1)}, u32[]{:S(2)}, u32[]{:S(2)}) async-start(f32[4,160,128]{2,1,0:T(8,128)} %bitcast.18), calls=%async_computation | async-start | bytes 655360 | tf_op jit(solution)/shard_map/cond/branch_0_fun/all_to_all | solution.py:226
  18.7 1.9 %all-gather.1 = f32[10,2,1024]{2,1,0:T(2,128)S(1)} all-gather(f32[5,2,1024]{2,1,0:T(2,128)S(1)} %get-tuple-element.59), channel_id=3, replica_groups={{0,1},{2,3},{4,5},{6,7},{8,9},{10,11},{12,13},{14,15},{16,17},{18,19},{..., dimensions={0}, use_global_device_ids=true | all-gather | bytes 122880 | tf_op jit(solution)/shard_map/cond/branch_0_fun/all_gather | solution.py:214
  20.5 0.3 %along.3 = f32[5,4,1024]{2,1,0:T(4,128)S(1)} custom-call(f32[5,32,128]{2,1,0:T(8,128)S(1)} %bitcast.76, f32[5,32,128]{2,1,0:T(8,128)S(1)} %get-tuple-element.56.inner_ref, f32[15,5,32,128]{3,2,1,0:T(8,128)S(1)} %bitcast.78, f32[5,32,128]{2,1,0:T(8,128)S(1)} %bitcast.80, f32[2,5,2,1024]{3,2,1,0:T(2,128)S(1)} %bitcast.66, ...), custom_call_target="tpu_custom_call" | custom-call | flops 1000000000 | tf_op jit(solution)/shard_map/cond/branch_0_fun/along/pallas_call | solution.py:215
  20.8 3.4 %all-to-all-done = f32[4,160,128]{2,1,0:T(8,128)S(1)} async-done(((f32[4,160,128]{2,1,0:T(8,128)}), f32[4,160,128]{2,1,0:T(8,128)S(1)}, u32[]{:S(2)}, u32[]{:S(2)}) %all-to-all-start) | async-done | bytes 327712 | tf_op jit(solution)/shard_map/cond/branch_0_fun/all_to_all | solution.py:226
  24.3 0.0 collective-permute-done.1.far_ref
  24.3 0.0 copy-done.1
  24.3 0.9 %finish.1 = f32[5,4,1024]{2,1,0:T(4,128)} custom-call(f32[5,4,1024]{2,1,0:T(4,128)S(1)} %get-tuple-element.72.part_ref, f32[4,5,4,1024]{3,2,1,0:T(4,128)S(1)} %get-tuple-element.73.spec_ref, f32[4,1024]{1,0:T(4,128)S(1)} %copy-done.1, f32[5,2,1024]{2,1,0:T(2,128)S(1)} %collective-permute-done.1.far_ref, s32[1,1024]{1,0:T(1,128)S(1)} %copy-done.3, ...), custom_call_target="tpu_custom_call" | custom-call | flops 409600 | bytes 409600 | tf_op jit(solution)/shard_map/finish/pallas_call | solution.py:245
  (3 shorter events, 0.0 us)
Async XLA Ops:
  0.0 4.9 %copy-start = (f32[1,4,5,5,4,1024]{5,4,3,2,1,0:T(4,128)S(1)}, f32[1,4,5,5,4,1024]{5,4,3,2,1,0:T(4,128)}, u32[]{:S(2)}) copy-start(f32[1,4,5,5,4,1024]{5,4,3,2,1,0:T(4,128)} %param.12) | copy-start | bytes 4915204
  0.0 5.0 %copy-start.2 = (f32[1,5,4,1024]{3,2,1,0:T(4,128)S(1)}, f32[1,5,4,1024]{3,2,1,0:T(4,128)}, u32[]{:S(2)}) copy-start(f32[1,5,4,1024]{3,2,1,0:T(4,128)} %param.11) | copy-start | bytes 245764
  0.0 13.9 %collective-permute-start = (f32[5,4,1024]{2,1,0:T(4,128)}, f32[5,4,1024]{2,1,0:T(4,128)S(1)}, u32[]{:S(2)}, u32[]{:S(2)}) collective-permute-start(f32[5,4,1024]{2,1,0:T(4,128)} %bitcast.70), channel_id=1, source_target_pairs={{0,64},{64,0},{128,192},{192,128},{256,320},{320,256},{384,448},{4... | collective-permute-start | bytes 245768 | tf_op jit(solution)/shard_map/ppermute | solution.py:202
  4.9 8.9 %copy-start.3 = (s32[1,1024]{1,0:T(1,128)S(1)}, s32[1,1024]{1,0:T(1,128)}, u32[]{:S(2)}) copy-start(s32[1,1024]{1,0:T(1,128)} %low_ref.1) | copy-start | bytes 12292
  4.9 8.9 %copy-start.4 = (s32[1,1024]{1,0:T(1,128)S(1)}, s32[1,1024]{1,0:T(1,128)}, u32[]{:S(2)}) copy-start(s32[1,1024]{1,0:T(1,128)} %up_ref.1) | copy-start | bytes 12292
  4.9 8.9 %copy-start.5 = (f32[1,3,5,5,4,1024]{5,4,3,2,1,0:T(4,128)S(1)}, f32[1,3,5,5,4,1024]{5,4,3,2,1,0:T(4,128)}, u32[]{:S(2)}) copy-start(f32[1,3,5,5,4,1024]{5,4,3,2,1,0:T(4,128)} %param.13) | copy-start | bytes 3686404
  4.9 8.9 %copy-start.6 = (f32[1,5,4,1024]{3,2,1,0:T(4,128)S(1)}, f32[1,5,4,1024]{3,2,1,0:T(4,128)}, u32[]{:S(2)}) copy-start(f32[1,5,4,1024]{3,2,1,0:T(4,128)} %param.14) | copy-start | bytes 245764
  5.2 19.1 %collective-permute-start.1 = (f32[5,2,1024]{2,1,0:T(2,128)S(1)}, f32[5,2,1024]{2,1,0:T(2,128)S(1)}, u32[]{:S(2)}, u32[]{:S(2)}) collective-permute-start(f32[5,2,1024]{2,1,0:T(2,128)S(1)} %get-tuple-element.74), channel_id=1, source_target_pairs={{1,2},{2,1},{3,4},{4,3},{5,6},{6,5},{7,8},{8,7},{9,10},{10,9},{11,... | collective-permute-start | bytes 122888 | tf_op jit(solution)/shard_map/ppermute | solution.py:209
  13.9 10.4 %copy-start.1 = (f32[4,1024]{1,0:T(4,128)S(1)}, f32[4,1024]{1,0:T(4,128)}, u32[]{:S(2)}) copy-start(f32[4,1024]{1,0:T(4,128)} %vol_ref.1) | copy-start | bytes 49156
  14.7 9.6 %all-to-all-start = ((f32[4,160,128]{2,1,0:T(8,128)}), f32[4,160,128]{2,1,0:T(8,128)S(1)}, u32[]{:S(2)}, u32[]{:S(2)}) async-start(f32[4,160,128]{2,1,0:T(8,128)} %bitcast.18), calls=%async_computation | async-start | bytes 655360 | tf_op jit(solution)/shard_map/cond/branch_0_fun/all_to_all | solution.py:226
